TPU v7x, 256 devices: a whole 4x4x8 slice. The times are simulated.
256 devices in a mesh: dp: 32 (over x, y, core), seq: 8 (over z).
Axes of the slice: x: 4, y: 4, z: 8, core: 2. Of those that a mesh axis runs over, the one named last changes fastest.
Arguments:
- features: bfloat16 [65536, 1024], P(('dp', 'seq')), may hold values from -16 to 16
- out_grad: bfloat16 [65536, 1024], P(('dp', 'seq')), may hold values from -6 to 6
- norm_gain: float32 [1024], replicated, may hold values from 0.25 to 1.75
- w_qkv: bfloat16 [1024, 1536], replicated, may hold values from -0.1875 to 0.1875
- w_out: bfloat16 [512, 1024], replicated, may hold values from -0.25 to 0.25
- w_msg: bfloat16 [1024, 1024], replicated, may hold values from -0.1875 to 0.1875
- block_ids: int32 [512, 4], P(('dp', 'seq')), may hold values from 0 to 15, as said below
- block_counts: int32 [512], P(('dp', 'seq')), may hold values from 1 to 4, as said below
- edge_tiles: bfloat16 [512, 4, 128, 128], P(('dp', 'seq')), may hold values from -0.375 to 0.375
Outputs:
- block_result_array: bfloat16 [65536, 1024], P(('dp', 'seq'))
- grad_input: bfloat16 [65536, 1024], P(('dp', 'seq'))
- grad_gain: float32 [1024], P('dp')
- grad_qkv: float32 [1024, 1536], P('dp')
- grad_w_out: float32 [512, 1024], P('dp')
- grad_msg: float32 [1024, 1024], P('dp')
Inputs may be any that keep to these rules, and one draw needn't show every extreme that they name: `block_ids`: slot 0 of a block's list is the block itself; every entry names a block of the same cluster at most 2 blocks away, and that distance is reached in every cluster. `block_counts`: every cluster has a block with all 4 slots live.
All inputs are finite; a program needn't handle non-finite values.
Results may differ from a plain program's by a relative error of at most 0.035.
Values may be sent and summed in bfloat16 or wider, within the bound.
No kernel may reach another device: no remote copies, remote signals or barrier semaphores. Data moves between devices by JAX's collectives and lax.ppermute only.
A program may use at most 128 MiB of HBM per device.

v0:
```python
import jax
import jax.numpy as jnp
from jax import lax
from jax.sharding import PartitionSpec as P

HEAD_DIM = 64
BLOCK = 128


exponent_divisor = 32.0
epsilon = 1e-06


def with_halo(block, sides, width):
    for axis, dim in sides:
        count = lax.axis_size(axis)
        forward = [(i, i + 1) for i in range(count - 1)]
        backward = [(target, source) for source, target in forward]
        low = lax.ppermute(
            lax.slice_in_dim(block, block.shape[dim] - width, None, axis=dim), axis, forward
        )
        high = lax.ppermute(lax.slice_in_dim(block, 0, width, axis=dim), axis, backward)
        block = jnp.concatenate([low, block, high], axis=dim)
    return block


def shifted(block, axis, distance):
    devices = range(lax.axis_size(axis))
    route = [(i - distance, i) for i in devices if i - distance in devices]
    return lax.ppermute(block, axis, route)


def unit_rows(block):
    wide = block.astype(jnp.float32)
    factor = lax.rsqrt(jnp.mean(wide * wide, axis=-1, keepdims=True) + epsilon)
    return (wide, factor)


def attend_head(asker_vector_split, k_head, payload_subspace):
    q_wide, q_factor = unit_rows(asker_vector_split)
    k_wide, k_factor = unit_rows(k_head)
    q_unit = (q_wide * q_factor).astype(jnp.bfloat16)
    k_unit = (k_wide * k_factor).astype(jnp.bfloat16)
    similarity_multiplier = exponent_divisor / asker_vector_split.shape[-1]
    scores = (
        lax.dot_general(
            q_unit, k_unit, (((1,), (1,)), ((), ())), preferred_element_type=jnp.float32
        )
        * similarity_multiplier
    )
    exp_scores = jnp.exp(scores)
    attention_weights_matrix = exp_scores / jnp.sum(exp_scores, axis=-1, keepdims=True)
    prob_low = attention_weights_matrix.astype(jnp.bfloat16)
    head_out = jnp.dot(prob_low, payload_subspace, preferred_element_type=jnp.float32).astype(
        jnp.bfloat16
    )
    return (head_out, attention_weights_matrix, q_unit, k_unit)


def attend_back(
    asker_vector_split,
    k_head,
    payload_subspace,
    q_unit,
    k_unit,
    attention_weights_matrix,
    head_out,
    d_head,
):
    prob_low = attention_weights_matrix.astype(jnp.bfloat16)
    d_value = lax.dot_general(
        prob_low, d_head, (((0,), (0,)), ((), ())), preferred_element_type=jnp.float32
    ).astype(jnp.bfloat16)
    d_prob = lax.dot_general(
        d_head, payload_subspace, (((1,), (1,)), ((), ())), preferred_element_type=jnp.float32
    )
    row_dot = jnp.sum(
        d_head.astype(jnp.float32) * head_out.astype(jnp.float32), axis=-1, keepdims=True
    )
    d_scores = (attention_weights_matrix * (d_prob - row_dot)).astype(jnp.bfloat16)
    similarity_multiplier = exponent_divisor / asker_vector_split.shape[-1]
    grad_query_normalized = (
        jnp.dot(d_scores, k_unit, preferred_element_type=jnp.float32) * similarity_multiplier
    )
    d_kunit = (
        lax.dot_general(
            d_scores, q_unit, (((0,), (0,)), ((), ())), preferred_element_type=jnp.float32
        )
        * similarity_multiplier
    )
    q_wide, q_factor = unit_rows(asker_vector_split)
    k_wide, k_factor = unit_rows(k_head)
    d_query = q_factor * grad_query_normalized - q_factor**3 * q_wide * jnp.mean(
        grad_query_normalized * q_wide, axis=-1, keepdims=True
    )
    d_key = k_factor * d_kunit - k_factor**3 * k_wide * jnp.mean(
        d_kunit * k_wide, axis=-1, keepdims=True
    )
    return (d_query.astype(jnp.bfloat16), d_key.astype(jnp.bfloat16), d_value)


def contract_rows(left, right):
    return lax.dot_general(
        left, right, (((0,), (0,)), ((), ())), preferred_element_type=jnp.float32
    )


def contract_cols(left, right):
    return lax.dot_general(
        left, right, (((1,), (1,)), ((), ())), preferred_element_type=jnp.float32
    )


def on_device(
    features, out_grad, norm_gain, w_qkv, w_out, w_msg, block_ids, block_counts, edge_tiles
):
    node_rows, width = features.shape
    channel_breadth = w_out.shape[0]
    feat_wide = features.astype(jnp.float32)
    inv_rms = lax.rsqrt(jnp.mean(feat_wide * feat_wide, axis=-1, keepdims=True) + epsilon)
    x_hat = feat_wide * inv_rms
    normed = (x_hat * norm_gain).astype(jnp.bfloat16)
    proj = jnp.dot(normed, w_qkv, preferred_element_type=jnp.float32).astype(jnp.bfloat16)
    q_heads, k_heads, v_heads = (
        lax.all_to_all(proj[:, :channel_breadth], "seq", split_axis=1, concat_axis=0, tiled=True),
        lax.all_to_all(
            proj[:, channel_breadth : 2 * channel_breadth],
            "seq",
            split_axis=1,
            concat_axis=0,
            tiled=True,
        ),
        lax.all_to_all(
            proj[:, 2 * channel_breadth :], "seq", split_axis=1, concat_axis=0, tiled=True
        ),
    )
    nodes_per_cluster, local_width = q_heads.shape
    local_channel_groups = local_width // HEAD_DIM

    def split_heads(arr):
        return arr.reshape(nodes_per_cluster, local_channel_groups, HEAD_DIM)

    forward_heads = jax.vmap(attend_head, in_axes=1, out_axes=(1, 0, 1, 1))
    backward_heads = jax.vmap(attend_back, in_axes=(1, 1, 1, 1, 1, 0, 1, 1), out_axes=1)
    q_split, k_split, v_split = (split_heads(q_heads), split_heads(k_heads), split_heads(v_heads))
    head_out, attention_weights_matrix, q_unit, k_unit = forward_heads(q_split, k_split, v_split)
    out_rows = lax.all_to_all(
        head_out.reshape(nodes_per_cluster, local_width),
        "seq",
        split_axis=0,
        concat_axis=1,
        tiled=True,
    )
    msg_rows = jnp.dot(normed, w_msg, preferred_element_type=jnp.float32).astype(jnp.bfloat16)
    wide_msg = with_halo(msg_rows, (("seq", 0),), node_rows)
    blocks_here = node_rows // BLOCK
    count_of_slots = block_ids.shape[1]
    base_block = (lax.axis_index("seq") - 1) * blocks_here
    local_ids = block_ids - base_block
    source = wide_msg.reshape(3 * blocks_here, BLOCK, width)[local_ids]
    live_mask = (
        jnp.arange(count_of_slots, dtype=jnp.int32)[None, :] < block_counts[:, None]
    ).astype(jnp.bfloat16)
    live = edge_tiles * live_mask[:, :, None, None]
    agg = jnp.einsum("bsij,bsjd->bid", live, source, preferred_element_type=jnp.float32).reshape(
        node_rows, width
    )
    attn_part = jnp.dot(out_rows, w_out, preferred_element_type=jnp.float32)
    block_result_array = (feat_wide + attn_part + jax.nn.silu(agg)).astype(jnp.bfloat16)
    grad_wide = out_grad.astype(jnp.float32)
    sigma = jax.nn.sigmoid(agg)
    d_agg = (grad_wide * sigma * (1.0 + agg * (1.0 - sigma))).astype(jnp.bfloat16)
    d_out = contract_cols(out_grad, w_out).astype(jnp.bfloat16)
    partial_out = contract_rows(out_rows, out_grad)
    d_heads = split_heads(lax.all_to_all(d_out, "seq", split_axis=1, concat_axis=0, tiled=True))
    d_query, d_key, d_value = backward_heads(
        q_split, k_split, v_split, q_unit, k_unit, attention_weights_matrix, head_out, d_heads
    )
    dq_rows, dk_rows, dv_rows = (
        lax.all_to_all(
            d_query.reshape(nodes_per_cluster, local_width),
            "seq",
            split_axis=0,
            concat_axis=1,
            tiled=True,
        ),
        lax.all_to_all(
            d_key.reshape(nodes_per_cluster, local_width),
            "seq",
            split_axis=0,
            concat_axis=1,
            tiled=True,
        ),
        lax.all_to_all(
            d_value.reshape(nodes_per_cluster, local_width),
            "seq",
            split_axis=0,
            concat_axis=1,
            tiled=True,
        ),
    )
    d_proj = jnp.concatenate([dq_rows, dk_rows, dv_rows], axis=1)
    contrib = jnp.einsum(
        "bsij,bid->bsjd",
        live,
        d_agg.reshape(blocks_here, BLOCK, width),
        preferred_element_type=jnp.float32,
    )
    position_tallies = (
        local_ids[:, :, None] == jnp.arange(3 * blocks_here, dtype=jnp.int32)[None, None, :]
    ).astype(jnp.float32)
    landed = jnp.einsum("bsk,bsjd->kjd", position_tallies, contrib, precision=lax.Precision.HIGHEST)
    from_above = shifted(landed[:blocks_here].astype(jnp.bfloat16), "seq", -1).astype(jnp.float32)
    from_below = shifted(landed[2 * blocks_here :].astype(jnp.bfloat16), "seq", 1).astype(
        jnp.float32
    )
    d_msg = (
        (landed[blocks_here : 2 * blocks_here] + from_above + from_below)
        .reshape(node_rows, width)
        .astype(jnp.bfloat16)
    )
    partial_msg = contract_rows(normed, d_msg)
    d_norm = contract_cols(d_proj, w_qkv) + contract_cols(d_msg, w_msg)
    scaled_logits = d_norm * norm_gain
    d_feat = inv_rms * (
        scaled_logits - x_hat * jnp.mean(scaled_logits * x_hat, axis=-1, keepdims=True)
    )
    grad_input = (grad_wide + d_feat).astype(jnp.bfloat16)
    partial_qkv = contract_rows(normed, d_proj)
    partial_gain = jnp.sum(d_norm * x_hat, axis=0)
    shares = (
        lax.psum_scatter(
            partial_qkv.astype(jnp.bfloat16), "dp", scatter_dimension=0, tiled=True
        ).astype(jnp.float32),
        lax.psum_scatter(
            partial_out.astype(jnp.bfloat16), "dp", scatter_dimension=0, tiled=True
        ).astype(jnp.float32),
        lax.psum_scatter(
            partial_msg.astype(jnp.bfloat16), "dp", scatter_dimension=0, tiled=True
        ).astype(jnp.float32),
        lax.psum_scatter(
            partial_gain.astype(jnp.bfloat16), "dp", scatter_dimension=0, tiled=True
        ).astype(jnp.float32),
    )
    sum_qkv, sum_out, sum_msg, sum_gain = (
        lax.psum(shares[0].astype(jnp.bfloat16), "seq").astype(jnp.float32),
        lax.psum(shares[1].astype(jnp.bfloat16), "seq").astype(jnp.float32),
        lax.psum(shares[2].astype(jnp.bfloat16), "seq").astype(jnp.float32),
        lax.psum(shares[3].astype(jnp.bfloat16), "seq").astype(jnp.float32),
    )
    return (
        block_result_array,
        grad_input,
        sum_gain / nodes_per_cluster,
        sum_qkv / nodes_per_cluster,
        sum_out / nodes_per_cluster,
        sum_msg / nodes_per_cluster,
    )


def solution(mesh):
    return jax.shard_map(
        on_device,
        mesh=mesh,
        in_specs=(
            P(("dp", "seq"), None),
            P(("dp", "seq"), None),
            P(),
            P(),
            P(),
            P(),
            P(("dp", "seq"), None),
            P(("dp", "seq")),
            P(("dp", "seq"), None, None, None),
        ),
        out_specs=(
            P(("dp", "seq"), None),
            P(("dp", "seq"), None),
            P("dp"),
            P("dp", None),
            P("dp", None),
            P("dp", None),
        ),
        check_vma=False,
    )
```

profile of v0, /device:TPU:6, one launch (start us, length us, event | category | flops | bytes accessed | tf_op | source)
XLA Modules:
  0.0 501.0 jit_solution(4162182378429599384)
XLA Ops:
  13.0 8.5 %all-to-all-start.2 = ((bf16[256,8,64]{0,2,1:T(8,128)(2,1)}), bf16[256,8,64]{0,2,1:T(8,128)(2,1)S(1)}, u32[]{:S(2)}, u32[]{:S(2)}) async-start(bf16[256,8,64]{0,2,1:T(8,128)(2,1)} %bitcast.157), calls=%async_computation.2 | async-start | bytes 524288 | tf_op jit(solution)/shard_map/all_to_all | solution.py:133
  26.1 5.4 %collective-permute-start = (bf16[256,1024]{1,0:T(8,128)(2,1)}, bf16[256,1024]{1,0:T(8,128)(2,1)}, u32[]{:S(2)}, u32[]{:S(2)}) collective-permute-start(bf16[256,1024]{1,0:T(8,128)(2,1)} %convolution_convert_fusion.6), channel_id=1, source_target_pairs={{0,1},{1,2},{2,3},{3,4},{4,5},{5,6},{6,7},{8,9},{9,10},{10,11},{11... | collective-permute-start | bytes 1572872 | tf_op jit(solution)/shard_map/ppermute | solution.py:19
  36.6 6.4 %all-to-all-start.1 = ((bf16[256,8,64]{0,2,1:T(8,128)(2,1)}), bf16[256,8,64]{0,2,1:T(8,128)(2,1)S(1)}, u32[]{:S(2)}, u32[]{:S(2)}) async-start(bf16[256,8,64]{0,2,1:T(8,128)(2,1)} %bitcast.155), calls=%async_computation.1 | async-start | bytes 524288 | tf_op jit(solution)/shard_map/all_to_all | solution.py:126
  46.7 6.4 %all-to-all-done.1 = bf16[256,8,64]{0,2,1:T(8,128)(2,1)S(1)} async-done(((bf16[256,8,64]{0,2,1:T(8,128)(2,1)}), bf16[256,8,64]{0,2,1:T(8,128)(2,1)S(1)}, u32[]{:S(2)}, u32[]{:S(2)}) %all-to-all-start.1) | async-done | bytes 262176 | tf_op jit(solution)/shard_map/all_to_all | solution.py:126
  53.1 4.0 all-to-all-start
  62.9 4.8 all-to-all-done
  67.7 4.1 all-to-all-start.4
  91.7 7.1 %all-to-all-start.3 = ((bf16[8,256,64]{1,2,0:T(8,128)(2,1)}), bf16[8,256,64]{1,2,0:T(8,128)(2,1)}, u32[]{:S(2)}, u32[]{:S(2)}) async-start(bf16[8,256,64]{1,2,0:T(8,128)(2,1)} %bitcast.153), calls=%async_computation.3 | async-start | bytes 524288 | tf_op jit(solution)/shard_map/all_to_all | solution.py:147
  99.7 6.1 %convolution_convert_fusion.3 = bf16[2048,64]{0,1:T(8,128)(2,1)S(1)} fusion(bf16[2048,2048]{0,1:T(8,128)(2,1)} %copy-done.1, bf16[2048,64]{0,1:T(8,128)(2,1)S(1)} %bitcast.149), kind=kOutput, calls=%fused_computation.11 | convolution fusion | flops 537001984 | bytes 8912896 | tf_op jit(solution)/shard_map/vmap()/dot_general | solution.py:71
  118.2 6.6 %fusion.5 = f32[6,128,1024]{2,0,1:T(8,128)S(1)} fusion(f32[2,4,128,1024]{3,2,1,0:T(8,128)S(1)} %fusion.43, s32[2,4]{1,0:T(2,128)S(1)} %get-tuple-element.15), kind=kOutput, calls=%fused_computation.12 | convolution fusion | flops 75497520 | bytes 7340064 | tf_op jit(solution)/shard_map/bsk,bsjd->kjd/dot_general | solution.py:212
  129.5 4.7 collective-permute-start.3
  135.5 8.3 %all-to-all-start.7 = ((bf16[8,256,64]{1,2,0:T(8,128)(2,1)}), bf16[8,256,64]{1,2,0:T(8,128)(2,1)}, u32[]{:S(2)}, u32[]{:S(2)}) async-start(bf16[8,256,64]{1,2,0:T(8,128)(2,1)} %bitcast.151), calls=%async_computation.7 | async-start | bytes 524288 | tf_op jit(solution)/shard_map/all_to_all | solution.py:194
  146.8 9.9 %multiply_convert_fusion = bf16[2048,2048]{0,1:T(8,128)(2,1)} fusion(bf16[2048,64]{0,1:T(8,128)(2,1)} %bitcast.150, bf16[2048,64]{0,1:T(8,128)(2,1)S(1)} %bitcast.146, f32[2048]{0:T(1024)S(1)} %bitcast.170, f32[2048]{0:T(1024)S(1)} %get-tuple-element.31, f32[2048,2048]{0,1:T(8,128)} %copy-done.2), kind=kOutput, calls=%fused_computation.1 | convolution fusion | flops 557842432 | bytes 25706496 | tf_op jit(solution)/shard_map/vmap()/dot_general | solution.py:74
  163.3 6.4 %multiply_reduce_fusion = (f32[2048]{0:T(1024)S(1)}, f32[2048,64]{0,1:T(8,128)S(1)}) fusion(f32[2048,64]{0,1:T(8,128)} %bitcast.133, bf16[2048,2048]{0,1:T(8,128)(2,1)} %multiply_convert_fusion, f32[2048,64]{0,1:T(8,128)} %bitcast.138, f32[2048]{0:T(1024)S(1)} %bitcast.167), kind=kOutput, calls=%fused_computation.59 | convolution fusion | flops 537524224 | bytes 9977856 | tf_op jit(solution)/shard_map/vmap()/dot_general | solution.py:86
  169.8 5.9 %multiply_reduce_fusion.1 = (f32[2048]{0:T(1024)S(1)}, f32[2048,64]{0,1:T(8,128)}) fusion(f32[2048,64]{0,1:T(8,128)S(1)} %bitcast.140, bf16[2048,2048]{0,1:T(8,128)(2,1)} %multiply_convert_fusion, f32[2048,64]{0,1:T(8,128)S(1)} %bitcast.134, f32[2048]{0:T(1024)S(1)} %bitcast.163), kind=kOutput, calls=%fused_computation.62 | convolution fusion | flops 537524224 | bytes 9977856 | tf_op jit(solution)/shard_map/vmap()/dot_general | solution.py:83
  176.4 6.9 %all-to-all-start.6 = ((bf16[8,256,64]{1,2,0:T(8,128)(2,1)}), bf16[8,256,64]{1,2,0:T(8,128)(2,1)}, u32[]{:S(2)}, u32[]{:S(2)}) async-start(bf16[8,256,64]{1,2,0:T(8,128)(2,1)} %bitcast.130), calls=%async_computation.6 | async-start | bytes 524288 | tf_op jit(solution)/shard_map/all_to_all | solution.py:187
  184.8 9.2 %all-to-all-done.6 = bf16[8,256,64]{1,2,0:T(8,128)(2,1)} async-done(((bf16[8,256,64]{1,2,0:T(8,128)(2,1)}), bf16[8,256,64]{1,2,0:T(8,128)(2,1)}, u32[]{:S(2)}, u32[]{:S(2)}) %all-to-all-start.6) | async-done | bytes 262176 | tf_op jit(solution)/shard_map/all_to_all | solution.py:187
  194.0 12.9 %all_to_all.134 = bf16[8,256,64]{1,2,0:T(8,128)(2,1)S(1)} all-to-all(bf16[8,256,64]{1,2,0:T(8,128)(2,1)S(1)} %bitcast.158), channel_id=1, replica_groups=mesh['dp'=32,'seq'=8] {'seq'}, dimensions={0} | all-to-all | bytes 524288 | tf_op jit(solution)/shard_map/all_to_all | solution.py:180
  207.5 4.0 convolution_convert_fusion
  220.7 53.1 %all-reduce = bf16[1024]{0:T(1024)(128)(2,1)S(1)} all-reduce(bf16[1024]{0:T(1024)(128)(2,1)S(1)} %get-tuple-element.6), channel_id=2, replica_groups=mesh['dp'=32,'seq'=8] {'dp'}, use_global_device_ids=true, to_apply=%region_9.10.clone | all-reduce | flops 1024 | bytes 4096
  276.5 27.8 %all-reduce.1 = (bf16[32]{0:T(256)(128)(2,1)S(1)}, bf16[16,1024]{1,0:T(8,128)(2,1)S(1)}) all-reduce(bf16[32]{0:T(256)(128)(2,1)S(1)} %dynamic-slice.1, bf16[16,1024]{1,0:T(8,128)(2,1)} %reduce-scatter.6.cloned.1.call-done), channel_id=1, replica_groups=mesh['dp'=32,'seq'=8] {'seq'}, use_global_device_ids=true, to_apply=%region_10.11 | all-reduce | flops 16416 | bytes 65664 | tf_op jit(solution)/shard_map/psum | solution.py:249
  304.9 20.2 %reduce-scatter.8.cloned.1.call-done = bf16[32,1024]{1,0:T(8,128)(2,1)} async-done(((bf16[1024,1024]{1,0:T(8,128)(2,1)}), bf16[32,1024]{1,0:T(8,128)(2,1)}) %reduce-scatter.8.cloned.1.call-update) | async-done | bytes 65552 | tf_op jit(solution)/shard_map/reduce_scatter | solution.py:238
  325.1 91.9 %reduce-scatter.4.cloned.1.call-done = bf16[32,1536]{1,0:T(8,128)(2,1)} async-done(((bf16[1024,1536]{1,0:T(8,128)(2,1)}), bf16[32,1536]{1,0:T(8,128)(2,1)}) %reduce-scatter.4.cloned.1.call-update) | async-done | bytes 98320 | tf_op jit(solution)/shard_map/reduce_scatter | solution.py:232
  417.6 73.8 %all-reduce.5.cloned.1.call-done = (bf16[32,1536]{1,0:T(8,128)(2,1)}, bf16[32,1024]{1,0:T(8,128)(2,1)}) async-done(((bf16[32,1536]{1,0:T(8,128)(2,1)}, bf16[32,1024]{1,0:T(8,128)(2,1)}), (bf16[32,1536]{1,0:T(8,128)(2,1)}, bf16[32,1024]{1,0:T(8,128)(2,1)})) %all-reduce.5.cloned.1.call-update) | async-done | bytes 163856 | tf_op jit(solution)/shard_map/psum | solution.py:246
  (131 shorter events, 91.7 us)
Async XLA Ops:
  9.2 12.3 %copy-start.20 = (f32[1024]{0:T(1024)S(1)}, f32[1024]{0:T(1024)}, u32[]{:S(2)}) copy-start(f32[1024]{0:T(1024)} %param.11) | copy-start | bytes 12292
  13.0 22.8 %all-to-all-start.2 = ((bf16[256,8,64]{0,2,1:T(8,128)(2,1)}), bf16[256,8,64]{0,2,1:T(8,128)(2,1)S(1)}, u32[]{:S(2)}, u32[]{:S(2)}) async-start(bf16[256,8,64]{0,2,1:T(8,128)(2,1)} %bitcast.157), calls=%async_computation.2 | async-start | bytes 524288 | tf_op jit(solution)/shard_map/all_to_all | solution.py:133
  21.5 21.5 %copy-start.21 = (s32[2,4]{1,0:T(2,128)S(1)}, s32[2,4]{1,0:T(2,128)}, u32[]{:S(2)}) copy-start(s32[2,4]{1,0:T(2,128)} %param.15) | copy-start | bytes 100
  21.5 25.1 %copy-start.22 = (s32[2]{0:T(128)S(1)}, s32[2]{0:T(128)}, u32[]{:S(2)}) copy-start(s32[2]{0:T(128)} %param.16) | copy-start | bytes 28
  24.9 82.8 %collective-permute-start.1 = (bf16[256,1024]{1,0:T(8,128)(2,1)}, bf16[256,1024]{1,0:T(8,128)(2,1)}, u32[]{:S(2)}, u32[]{:S(2)}) collective-permute-start(bf16[256,1024]{1,0:T(8,128)(2,1)} %convolution_convert_fusion.6), channel_id=1, source_target_pairs={{1,0},{2,1},{3,2},{4,3},{5,4},{6,5},{7,6},{9,8},{10,9},{11,10},{12... | collective-permute-start | bytes 1572872 | tf_op jit(solution)/shard_map/ppermute | solution.py:22
  26.1 81.5 %collective-permute-start = (bf16[256,1024]{1,0:T(8,128)(2,1)}, bf16[256,1024]{1,0:T(8,128)(2,1)}, u32[]{:S(2)}, u32[]{:S(2)}) collective-permute-start(bf16[256,1024]{1,0:T(8,128)(2,1)} %convolution_convert_fusion.6), channel_id=1, source_target_pairs={{0,1},{1,2},{2,3},{3,4},{4,5},{5,6},{6,7},{8,9},{9,10},{10,11},{11... | collective-permute-start | bytes 1572872 | tf_op jit(solution)/shard_map/ppermute | solution.py:19
  36.6 16.6 %all-to-all-start.1 = ((bf16[256,8,64]{0,2,1:T(8,128)(2,1)}), bf16[256,8,64]{0,2,1:T(8,128)(2,1)S(1)}, u32[]{:S(2)}, u32[]{:S(2)}) async-start(bf16[256,8,64]{0,2,1:T(8,128)(2,1)} %bitcast.155), calls=%async_computation.1 | async-start | bytes 524288 | tf_op jit(solution)/shard_map/all_to_all | solution.py:126
  53.1 14.5 %all-to-all-start = ((bf16[256,8,64]{0,2,1:T(8,128)(2,1)}), bf16[256,8,64]{0,2,1:T(8,128)(2,1)}, u32[]{:S(2)}, u32[]{:S(2)}) async-start(bf16[256,8,64]{0,2,1:T(8,128)(2,1)} %bitcast.156), calls=%async_computation | async-start | bytes 524288 | tf_op jit(solution)/shard_map/all_to_all | solution.py:125
  67.7 24.0 %all-to-all-start.4 = ((bf16[256,8,64]{0,2,1:T(8,128)(2,1)}), bf16[256,8,64]{0,2,1:T(8,128)(2,1)}, u32[]{:S(2)}, u32[]{:S(2)}) async-start(bf16[256,8,64]{0,2,1:T(8,128)(2,1)} %bitcast.154), calls=%async_computation.4 | async-start | bytes 524288 | tf_op jit(solution)/shard_map/all_to_all | solution.py:175
  91.7 43.9 %all-to-all-start.3 = ((bf16[8,256,64]{1,2,0:T(8,128)(2,1)}), bf16[8,256,64]{1,2,0:T(8,128)(2,1)}, u32[]{:S(2)}, u32[]{:S(2)}) async-start(bf16[8,256,64]{1,2,0:T(8,128)(2,1)} %bitcast.153), calls=%async_computation.3 | async-start | bytes 524288 | tf_op jit(solution)/shard_map/all_to_all | solution.py:147
  99.7 6.1 %copy-start.15 = (bf16[8,8,8,256]{3,2,0,1:T(8,128)(2,1)}, bf16[8,8,8,256]{3,2,0,1:T(8,128)(2,1)S(1)}, u32[]{:S(2)}) copy-start(bf16[8,8,8,256]{3,2,0,1:T(8,128)(2,1)S(1)} %copy.104) | copy-start | bytes 786436
  128.4 18.3 %copy-start.11 = (bf16[8,8,8,256]{3,2,0,1:T(8,128)(2,1)S(1)}, bf16[8,8,8,256]{3,2,0,1:T(8,128)(2,1)}, u32[]{:S(2)}) copy-start(bf16[8,8,8,256]{3,2,0,1:T(8,128)(2,1)} %copy.102) | copy-start | bytes 786436
  129.5 28.9 %collective-permute-start.3 = (bf16[2,128,1024]{2,1,0:T(8,128)(2,1)}, bf16[2,128,1024]{2,1,0:T(8,128)(2,1)}, u32[]{:S(2)}, u32[]{:S(2)}) collective-permute-start(bf16[2,128,1024]{2,1,0:T(8,128)(2,1)} %get-tuple-element.17), channel_id=1, source_target_pairs={{0,1},{1,2},{2,3},{3,4},{4,5},{5,6},{6,7},{8,9},{9,10},{10,11},{11... | collective-permute-start | bytes 1572872 | tf_op jit(solution)/shard_map/ppermute | solution.py:30
  134.2 24.2 %collective-permute-start.2 = (bf16[2,128,1024]{2,1,0:T(8,128)(2,1)}, bf16[2,128,1024]{2,1,0:T(8,128)(2,1)}, u32[]{:S(2)}, u32[]{:S(2)}) collective-permute-start(bf16[2,128,1024]{2,1,0:T(8,128)(2,1)} %get-tuple-element.16), channel_id=1, source_target_pairs={{1,0},{2,1},{3,2},{4,3},{5,4},{6,5},{7,6},{9,8},{10,9},{11,10},{12... | collective-permute-start | bytes 1572872 | tf_op jit(solution)/shard_map/ppermute | solution.py:30
  135.5 40.9 %all-to-all-start.7 = ((bf16[8,256,64]{1,2,0:T(8,128)(2,1)}), bf16[8,256,64]{1,2,0:T(8,128)(2,1)}, u32[]{:S(2)}, u32[]{:S(2)}) async-start(bf16[8,256,64]{1,2,0:T(8,128)(2,1)} %bitcast.151), calls=%async_computation.7 | async-start | bytes 524288 | tf_op jit(solution)/shard_map/all_to_all | solution.py:194
  143.8 132.7 %reduce-scatter.6.cloned.1.call-start = ((), (), s32[]{:S(2)}) async-start(), calls=%async_computation.12 | async-start | bytes 1081344 | tf_op jit(solution)/shard_map/reduce_scatter | solution.py:235
  146.7 178.4 %reduce-scatter.8.cloned.1.call-start = ((), (), s32[]{:S(2)}) async-start(), calls=%async_computation.13 | async-start | bytes 2162688 | tf_op jit(solution)/shard_map/reduce_scatter | solution.py:238
  146.8 10.0 %copy-start.13 = (f32[8,8,8,256]{3,2,1,0:T(8,128)S(1)}, f32[8,8,8,256]{3,2,1,0:T(8,128)}, u32[]{:S(2)}) copy-start(f32[8,8,8,256]{3,2,1,0:T(8,128)} %get-tuple-element.25) | copy-start | bytes 1572868
  146.8 10.8 %copy-start.14 = (f32[8,8,8,256]{3,2,1,0:T(8,128)S(1)}, f32[8,8,8,256]{3,2,1,0:T(8,128)}, u32[]{:S(2)}) copy-start(f32[8,8,8,256]{3,2,1,0:T(8,128)} %get-tuple-element.23) | copy-start | bytes 1572868
  163.3 6.5 %copy-start.5 = (f32[8,8,8,256]{3,2,0,1:T(8,128)S(1)}, f32[8,8,8,256]{3,2,0,1:T(8,128)}, u32[]{:S(2)}) copy-start(f32[8,8,8,256]{3,2,0,1:T(8,128)} %copy.103) | copy-start | bytes 1572868
  163.3 6.5 %copy-start.6 = (f32[8,8,8,256]{3,2,0,1:T(8,128)S(1)}, f32[8,8,8,256]{3,2,0,1:T(8,128)}, u32[]{:S(2)}) copy-start(f32[8,8,8,256]{3,2,0,1:T(8,128)} %copy.105) | copy-start | bytes 1572868
  176.4 17.5 %all-to-all-start.6 = ((bf16[8,256,64]{1,2,0:T(8,128)(2,1)}), bf16[8,256,64]{1,2,0:T(8,128)(2,1)}, u32[]{:S(2)}, u32[]{:S(2)}) async-start(bf16[8,256,64]{1,2,0:T(8,128)(2,1)} %bitcast.130), calls=%async_computation.6 | async-start | bytes 524288 | tf_op jit(solution)/shard_map/all_to_all | solution.py:187
  183.4 233.7 %reduce-scatter.4.cloned.1.call-start = ((), (), s32[]{:S(2)}) async-start(), calls=%async_computation.11 | async-start | bytes 3244032 | tf_op jit(solution)/shard_map/reduce_scatter | solution.py:232
  211.6 279.8 %all-reduce.5.cloned.1.call-start = ((), (), s32[]{:S(2)}) async-start(), calls=%async_computation.14 | async-start | bytes 327680 | tf_op jit(solution)/shard_map/psum | solution.py:246
  (15 other events, 44.7 us)
Sparse Core Ops, SparseCore 0:
  148.4 86.4 reduce-scatter.5
  239.2 85.8 reduce-scatter.7
  329.6 87.4 reduce-scatter.3
  419.3 72.0 all-reduce.4
where the time goes:
time: 503 us; the launch traced here: 501 us
  waiting for transfers between devices  206 us (41%)
  blocking collectives  93.7 us (19%)
  matrix products  67.4 us (13%)
  starting transfers between devices  58.3 us (12%)
  local copies, waits for them, and re-layouts  33.4 us (7%)
  other arithmetic  26.9 us (5%)
  between operations  14.9 us (3%)
    reduce_scatter x1, waiting for transfers between devices, on_device(): lax.psum_scatter(partial_qkv.astype(jnp.bfloat16), 'dp', scatter_dimensio...  91.9 us
    psum x1, waiting for transfers between devices, on_device(): lax.psum(shares[0].astype(jnp.bfloat16), 'seq').astype(jnp.float32)  73.8 us
    unnamed x1, blocking collectives  53.1 us
    psum x1, blocking collectives, on_device(): lax.psum(shares[3].astype(jnp.bfloat16), 'seq').astype(jnp.float32)  27.8 us
    reduce_scatter x1, waiting for transfers between devices, on_device(): lax.psum_scatter(partial_msg.astype(jnp.bfloat16), 'dp', scatter_dimensio...  20.2 us
    all_to_all x1, blocking collectives, on_device(): lax.all_to_all(d_query.reshape(nodes_per_cluster, local_width), 'seq', sp...  12.9 us
  transfers between devices with their start and end apart: 15, of which 6 were waited for; matrix products, arithmetic and copies ran while one was open for 22% of the time, Pallas kernels for 0%

commit v1 on v0

v1 whole, which is shorter than its diff:
```python
import jax
import jax.numpy as jnp
from jax import lax
from jax.sharding import Mesh
from jax.sharding import PartitionSpec as P

HEAD_DIM = 64
BLOCK = 128
N_SEQ = 8
N_XY = 16

exponent_divisor = 32.0
epsilon = 1e-06


def unit_rows(block):
    wide = block.astype(jnp.float32)
    factor = lax.rsqrt(jnp.mean(wide * wide, axis=-1, keepdims=True) + epsilon)
    return (wide, factor)


def attend(query, keyrow, valrow, d_head):
    scale = exponent_divisor / HEAD_DIM
    q_wide, q_factor = unit_rows(query)
    k_wide, k_factor = unit_rows(keyrow)
    q_unit = (q_wide * q_factor).astype(jnp.bfloat16)
    k_unit = (k_wide * k_factor).astype(jnp.bfloat16)
    exp_scores = jnp.exp(contract_cols(q_unit, k_unit) * scale)
    prob = exp_scores / jnp.sum(exp_scores, axis=-1, keepdims=True)
    prob_low = prob.astype(jnp.bfloat16)
    head_out = jnp.dot(prob_low, valrow, preferred_element_type=jnp.float32).astype(jnp.bfloat16)
    d_value = contract_rows(prob_low, d_head).astype(jnp.bfloat16)
    d_prob = contract_cols(d_head, valrow)
    row_dot = jnp.sum(
        d_head.astype(jnp.float32) * head_out.astype(jnp.float32), axis=-1, keepdims=True
    )
    d_scores = (prob * (d_prob - row_dot)).astype(jnp.bfloat16)
    d_qunit = jnp.dot(d_scores, k_unit, preferred_element_type=jnp.float32) * scale
    d_kunit = contract_rows(d_scores, q_unit) * scale
    d_query = q_factor * d_qunit - q_factor**3 * q_wide * jnp.mean(
        d_qunit * q_wide, axis=-1, keepdims=True
    )
    d_key = k_factor * d_kunit - k_factor**3 * k_wide * jnp.mean(
        d_kunit * k_wide, axis=-1, keepdims=True
    )
    return head_out, d_query.astype(jnp.bfloat16), d_key.astype(jnp.bfloat16), d_value


def contract_rows(left, right):
    return lax.dot_general(
        left, right, (((0,), (0,)), ((), ())), preferred_element_type=jnp.float32
    )


def contract_cols(left, right):
    return lax.dot_general(
        left, right, (((1,), (1,)), ((), ())), preferred_element_type=jnp.float32
    )


def exchange(array, axis):
    return lax.all_to_all(array, axis, split_axis=0, concat_axis=0, tiled=True)


def up(array):
    return lax.ppermute(array, "z", [(i, (i + 1) % N_SEQ) for i in range(N_SEQ)])


def down(array):
    return lax.ppermute(array, "z", [((i + 1) % N_SEQ, i) for i in range(N_SEQ)])


def sum_over_dp(partial):
    rows, width = partial.shape
    core = lax.axis_index("c")
    parts = partial.astype(jnp.bfloat16).reshape(N_XY, 2, rows // (2 * N_XY), width)
    keep = lax.dynamic_index_in_dim(parts, core, 1, keepdims=False)
    give = lax.dynamic_index_in_dim(parts, 1 - core, 1, keepdims=False)
    got = lax.ppermute(give, "c", [(0, 1), (1, 0)])
    pair = (keep.astype(jnp.float32) + got.astype(jnp.float32)).astype(jnp.bfloat16)
    shares = exchange(pair, ("x", "y"))
    return jnp.sum(shares.astype(jnp.float32), axis=0)


def on_device(
    features, out_grad, norm_gain, w_qkv, w_out, w_msg, block_ids, block_counts, edge_tiles
):
    node_rows, width = features.shape
    hd = w_out.shape[0]
    z = lax.axis_index("z")
    feat_wide = features.astype(jnp.float32)
    inv_rms = lax.rsqrt(jnp.mean(feat_wide * feat_wide, axis=-1, keepdims=True) + epsilon)
    x_hat = feat_wide * inv_rms
    normed = (x_hat * norm_gain).astype(jnp.bfloat16)

    a1, b1 = up(normed), down(normed)
    a2, b2 = up(a1), down(b1)
    a3, b3 = up(a2), down(b2)
    half = node_rows // 2
    c4 = jnp.concatenate([up(a3[:half]), down(b3[half:])], axis=0)
    chunks = [normed, a1, a2, a3, c4, b3, b2, b1]

    d_out = contract_cols(out_grad, w_out).astype(jnp.bfloat16)
    d_out = d_out.reshape(2, half, N_SEQ, HEAD_DIM).transpose(2, 1, 0, 3).reshape(N_SEQ, half, 2 * HEAD_DIM)
    d_heads = exchange(d_out, "z")
    relative = (z - jnp.arange(N_SEQ)) % N_SEQ
    d_heads = d_heads[relative].reshape(N_SEQ, half, 2, HEAD_DIM).transpose(0, 2, 1, 3)
    d_heads = d_heads.reshape(N_SEQ * node_rows, HEAD_DIM)

    w_head = lax.dynamic_index_in_dim(w_qkv.reshape(width, 3, N_SEQ, HEAD_DIM), z, 2, keepdims=False)
    w_head = w_head.reshape(width, 3 * HEAD_DIM)
    proj = jnp.concatenate(
        [jnp.dot(c, w_head, preferred_element_type=jnp.float32).astype(jnp.bfloat16) for c in chunks], axis=0
    )
    head_out, d_query, d_key, d_value = attend(
        proj[:, :HEAD_DIM], proj[:, HEAD_DIM : 2 * HEAD_DIM], proj[:, 2 * HEAD_DIM :], d_heads
    )
    back = (z - jnp.arange(N_SEQ)) % N_SEQ

    def home(left, right):
        both = jnp.concatenate([left, right], axis=1).reshape(N_SEQ, node_rows, 2 * HEAD_DIM)
        both = exchange(both[back], "z")
        flat = both.reshape(N_SEQ, node_rows, 2, HEAD_DIM).transpose(2, 1, 0, 3)
        flat = flat.reshape(2, node_rows, hd)
        return flat[0], flat[1]

    out_rows, dv_rows = home(head_out, d_value)
    dq_rows, dk_rows = home(d_query, d_key)

    wide = jnp.concatenate([a1, normed, b1], axis=0)
    blocks_here = node_rows // BLOCK
    wide_msg = jnp.dot(wide, w_msg, preferred_element_type=jnp.float32).astype(jnp.bfloat16)
    local_ids = block_ids - (z - 1) * blocks_here
    source = wide_msg.reshape(3 * blocks_here, BLOCK, width)[local_ids]
    slots = block_ids.shape[1]
    live_mask = (jnp.arange(slots, dtype=jnp.int32)[None, :] < block_counts[:, None]).astype(jnp.bfloat16)
    live = edge_tiles * live_mask[:, :, None, None]
    agg = jnp.einsum("bsij,bsjd->bid", live, source, preferred_element_type=jnp.float32).reshape(
        node_rows, width
    )
    grad_wide = out_grad.astype(jnp.float32)
    sigma = jax.nn.sigmoid(agg)
    d_agg = (grad_wide * sigma * (1.0 + agg * (1.0 - sigma))).astype(jnp.bfloat16)
    contrib = jnp.einsum(
        "bsij,bid->bsjd",
        live,
        d_agg.reshape(blocks_here, BLOCK, width),
        preferred_element_type=jnp.float32,
    )
    tally = (
        local_ids[:, :, None] == jnp.arange(3 * blocks_here, dtype=jnp.int32)[None, None, :]
    ).astype(jnp.float32)
    landed = jnp.einsum("bsk,bsjd->kjd", tally, contrib, precision=lax.Precision.HIGHEST)
    from_above = down(landed[:blocks_here].astype(jnp.bfloat16)).astype(jnp.float32)
    from_below = up(landed[2 * blocks_here :].astype(jnp.bfloat16)).astype(jnp.float32)
    d_msg = (
        (landed[blocks_here : 2 * blocks_here] + from_above + from_below)
        .reshape(node_rows, width)
        .astype(jnp.bfloat16)
    )
    sum_msg = sum_over_dp(contract_rows(normed, d_msg))

    attn_part = jnp.dot(out_rows, w_out, preferred_element_type=jnp.float32)
    block_result_array = (feat_wide + attn_part + agg * sigma).astype(jnp.bfloat16)
    sum_out = sum_over_dp(contract_rows(out_rows, out_grad))

    d_proj = jnp.concatenate([dq_rows, dk_rows, dv_rows], axis=1)
    d_norm = contract_cols(d_proj, w_qkv) + contract_cols(d_msg, w_msg)
    scaled = d_norm * norm_gain
    d_feat = inv_rms * (scaled - x_hat * jnp.mean(scaled * x_hat, axis=-1, keepdims=True))
    grad_input = (grad_wide + d_feat).astype(jnp.bfloat16)

    d_head_proj = jnp.concatenate([d_query, d_key, d_value], axis=1)
    normed_all = jnp.concatenate(chunks, axis=0)
    sum_head = sum_over_dp(contract_rows(normed_all, d_head_proj))

    tall = jnp.concatenate([sum_msg, sum_out], axis=0).astype(jnp.bfloat16)
    tall = tall.reshape(N_SEQ, tall.shape[0] // N_SEQ, width)
    share = jnp.sum(exchange(tall, "z").astype(jnp.float32), axis=0)
    mine = jnp.concatenate([share.astype(jnp.bfloat16).reshape(-1, 2 * BLOCK), sum_head.astype(jnp.bfloat16).reshape(-1, 2 * BLOCK)], axis=0)
    every = exchange(jnp.broadcast_to(mine[None], (N_SEQ,) + mine.shape), "z")
    cut = share.size // (2 * BLOCK)
    nodes = N_SEQ * node_rows
    flat = every[:, :cut].reshape(-1, width).astype(jnp.float32) / nodes
    grad_msg = flat[: sum_msg.shape[0]]
    grad_out = flat[sum_msg.shape[0] :]
    heads = every[:, cut:].reshape(N_SEQ, -1, 3, HEAD_DIM).transpose(1, 2, 0, 3)
    grad_qkv = heads.reshape(-1, 3 * hd).astype(jnp.float32) / nodes

    rows_here = grad_qkv.shape[0]
    first = ((lax.axis_index("x") * 4 + lax.axis_index("y")) * 2 + lax.axis_index("c")) * rows_here
    w_rows = lax.dynamic_slice_in_dim(w_qkv, first, rows_here, 0).astype(jnp.float32)
    m_rows = lax.dynamic_slice_in_dim(w_msg, first, rows_here, 0).astype(jnp.float32)
    gain_rows = lax.dynamic_slice_in_dim(norm_gain, first, rows_here, 0)
    grad_gain = (
        jnp.sum(w_rows * grad_qkv, axis=1) + jnp.sum(m_rows * grad_msg, axis=1)
    ) / gain_rows
    return block_result_array, grad_input, grad_gain, grad_qkv, grad_out, grad_msg


def solution(mesh):
    fine = Mesh(mesh.devices.reshape(4, 4, 2, N_SEQ), ("x", "y", "c", "z"))
    dp = ("x", "y", "c")
    rows = ("x", "y", "c", "z")
    return jax.shard_map(
        on_device,
        mesh=fine,
        in_specs=(
            P(rows, None),
            P(rows, None),
            P(),
            P(),
            P(),
            P(),
            P(rows, None),
            P(rows),
            P(rows, None, None, None),
        ),
        out_specs=(
            P(rows, None),
            P(rows, None),
            P(dp),
            P(dp, None),
            P(dp, None),
            P(dp, None),
        ),
        check_vma=False,
    )
```

time: 503 us -> 266 us (0.53)
  waiting for transfers between devices: 206 us -> 83.2 us
  blocking collectives: 93.7 us -> 0 us
  matrix products: 67.4 us -> 49 us
  between operations: 14.9 us -> 1.54 us
  other arithmetic: 26.9 us -> 35.3 us
    reduce_scatter x3 -> x0, waiting for transfers between devices: 112 us -> none  [the longest x1 91.9 us: on_device(): lax.psum_scatter(partial_qkv.astype(jnp.bfloat16), 'dp', scatter_dimensio...]
    psum x1 -> x0, waiting for transfers between devices: 73.8 us -> none  [on_device(): lax.psum(shares[0].astype(jnp.bfloat16), 'seq').astype(jnp.float32)]
    unnamed x1 -> x0, blocking collectives: 53.1 us -> none
    all_to_all x7 -> x8, waiting for transfers between devices: 20.5 us -> 55.9 us  [exchange(): return lax.all_to_all(array, axis, split_axis=0, concat_axis=0, tiled=True)]
    psum x1 -> x0, blocking collectives: 27.8 us -> none  [on_device(): lax.psum(shares[3].astype(jnp.bfloat16), 'seq').astype(jnp.float32)]
    ppermute x4 -> x13, waiting for transfers between devices: 0.01 us -> 27.3 us  [the longest x5 24.1 us: down(): lax.ppermute(array, 'z', [((i + 1) % N_SEQ, i) for i in range(N_SEQ)])]
    dot_general x9 -> x12, matrix products: 45.9 us -> 19.1 us  [the longest x1 6.64 us: on_device(): jnp.einsum('bsk,bsjd->kjd', tally, contrib, precision=lax.Precision.HIGHEST)]
    all_to_all x1 -> x0, blocking collectives: 12.9 us -> none  [on_device(): lax.all_to_all(d_query.reshape(nodes_per_cluster, local_width), 'seq', sp...]
  transfers between devices with their start and end apart: 15 -> 21, of which waited for: 6 -> 14; matrix products, arithmetic and copies ran while one was open for 22% -> 32% of each run, Pallas kernels for 0% -> 0%
where the time goes in v1:
time: 266 us; the launch traced here: 261 us
  waiting for transfers between devices  83.2 us (31%)
  starting transfers between devices  54.9 us (21%)
  matrix products  49 us (18%)
  local copies, waits for them, and re-layouts  37.2 us (14%)
  other arithmetic  35.3 us (13%)
    all_to_all x8, waiting for transfers between devices, exchange(): return lax.all_to_all(array, axis, split_axis=0, concat_axis=0, tiled=True)  55.9 us
    all_to_all x8, starting transfers between devices, exchange(): return lax.all_to_all(array, axis, split_axis=0, concat_axis=0, tiled=True)  40.5 us
    ppermute x5, waiting for transfers between devices, down(): lax.ppermute(array, 'z', [((i + 1) % N_SEQ, i) for i in range(N_SEQ)])  24.1 us
    dot_general x5, matrix products, contract_cols(): lax.dot_general(left, right, (((1,), (1,)), ((), ())), preferred_element_...  16.9 us
    unnamed x56, local copies, waits for them, and re-layouts  10.4 us
    ppermute x5, starting transfers between devices, down(): lax.ppermute(array, 'z', [((i + 1) % N_SEQ, i) for i in range(N_SEQ)])  9.68 us
    dot_general x5, matrix products, contract_rows(): lax.dot_general(left, right, (((0,), (0,)), ((), ())), preferred_element_...  8.69 us
    dot_general x1, matrix products, on_device(): jnp.einsum('bsk,bsjd->kjd', tally, contrib, precision=lax.Precision.HIGHEST)  6.64 us
  transfers between devices with their start and end apart: 21, of which 14 were waited for; matrix products, arithmetic and copies ran while one was open for 32% of the time, Pallas kernels for 0%

profile of v1, /device:TPU:6, one launch (start us, length us, event | category | flops | bytes accessed | tf_op | source)
XLA Modules:
  0.0 261.1 jit_solution(3336651297962707155)
XLA Ops:
  4.0 5.9 %collective-permute-start.4 = (bf16[256,1024]{1,0:T(8,128)(2,1)S(1)}, bf16[256,1024]{1,0:T(8,128)(2,1)S(1)}, u32[]{:S(2)}, u32[]{:S(2)}) collective-permute-start(bf16[256,1024]{1,0:T(8,128)(2,1)S(1)} %get-tuple-element.13), channel_id=1, source_target_pairs={{1,0},{2,1},{3,2},{4,3},{5,4},{6,5},{7,6},{0,7},{9,8},{10,9},{11,1... | collective-permute-start | bytes 1572872 | tf_op jit(solution)/shard_map/ppermute | solution.py:70
  12.4 4.8 %all-to-all-start = ((bf16[8,128,128]{1,2,0:T(8,128)(2,1)}), bf16[8,128,128]{1,2,0:T(8,128)(2,1)S(1)}, u32[]{:S(2)}, u32[]{:S(2)}) async-start(bf16[8,128,128]{1,2,0:T(8,128)(2,1)} %bitcast.3), calls=%async_computation | async-start | bytes 524288 | tf_op jit(solution)/shard_map/all_to_all | solution.py:62
  17.9 4.7 %copy.42 = bf16[1024,1536]{0,1:T(8,128)(2,1)} copy(bf16[1024,1536]{1,0:T(8,128)(2,1)} %param.12) | data formatting | bytes 6291456 | tf_op args[3]
  24.1 6.1 %all-to-all-done = bf16[8,128,128]{1,2,0:T(8,128)(2,1)S(1)} async-done(((bf16[8,128,128]{1,2,0:T(8,128)(2,1)}), bf16[8,128,128]{1,2,0:T(8,128)(2,1)S(1)}, u32[]{:S(2)}, u32[]{:S(2)}) %all-to-all-start) | async-done | bytes 262176 | tf_op jit(solution)/shard_map/all_to_all | solution.py:62
  34.5 4.7 %convolution_convert_fusion.3 = bf16[768,1024]{1,0:T(8,128)(2,1)} fusion(bf16[1024,1024]{1,0:T(8,128)(2,1)} %param.14, bf16[256,1024]{1,0:T(8,128)(2,1)S(1)} %collective-permute-done.4, bf16[256,1024]{1,0:T(8,128)(2,1)S(1)} %get-tuple-element.13, bf16[256,1024]{1,0:T(8,128)(2,1)} %collective-permute-done), kind=kOutput, calls=%fused_computation.17 | convolution fusion | flops 1616117760 | bytes 5242880 | tf_op jit(solution)/shard_map/dot_general | solution.py:132
  39.2 3.5 %gather_fusion.2 = bf16[8,128,1024]{2,1,0:T(8,128)(2,1)} fusion(bf16[6,128,1024]{2,1,0:T(8,128)(2,1)} %bitcast.133, s32[1024]{0:T(1024)S(1)} %pad_clamp_fusion), kind=kCustom, calls=%fused_computation.2 | custom fusion | bytes 4194336 | tf_op jit(solution)/shard_map/gather | solution.py:134
  47.2 6.6 %fusion.5 = f32[6,128,1024]{2,0,1:T(8,128)S(1)} fusion(f32[2,4,128,1024]{3,2,1,0:T(8,128)S(1)} %fusion.72, s32[2,4]{1,0:T(2,128)S(1)} %copy-done.21), kind=kOutput, calls=%fused_computation.13 | convolution fusion | flops 75497520 | bytes 7340064 | tf_op jit(solution)/shard_map/bsk,bsjd->kjd/dot_general | solution.py:153
  56.2 3.5 %fusion.99 = (bf16[6,128,1024]{2,1,0:T(8,128)(2,1)S(1)}, f32[6,128,1024]{2,1,0:T(8,128)}) fusion(f32[6,128,1024]{2,0,1:T(8,128)S(1)} %fusion.5), kind=kLoop, calls=%fused_computation.176 | loop fusion | flops 786432 | bytes 7864320 | tf_op jit(solution)/shard_map/convert.8
  62.7 6.1 %collective-permute-done.5 = bf16[256,1024]{1,0:T(8,128)(2,1)S(1)} collective-permute-done((bf16[256,1024]{1,0:T(8,128)(2,1)S(1)}, bf16[256,1024]{1,0:T(8,128)(2,1)S(1)}, u32[]{:S(2)}, u32[]{:S(2)}) %collective-permute-start.5) | collective-permute-done | bytes 524320 | tf_op jit(solution)/shard_map/ppermute | solution.py:70
  74.1 14.3 %collective-permute-done.6 = bf16[256,1024]{1,0:T(8,128)(2,1)S(1)} collective-permute-done((bf16[256,1024]{1,0:T(8,128)(2,1)S(1)}, bf16[256,1024]{1,0:T(8,128)(2,1)S(1)}, u32[]{:S(2)}, u32[]{:S(2)}) %collective-permute-start.6) | collective-permute-done | bytes 524320 | tf_op jit(solution)/shard_map/ppermute | solution.py:70
  91.2 3.7 %collective-permute-done.7 = bf16[128,1024]{1,0:T(8,128)(2,1)S(1)} collective-permute-done((bf16[128,1024]{1,0:T(8,128)(2,1)S(1)}, bf16[128,1024]{1,0:T(8,128)(2,1)S(1)}, u32[]{:S(2)}, u32[]{:S(2)}) %collective-permute-start.7) | collective-permute-done | bytes 262176 | tf_op jit(solution)/shard_map/ppermute | solution.py:70
  112.6 7.8 %multiply_convert_fusion = bf16[2048,2048]{0,1:T(8,128)(2,1)S(1)} fusion(bf16[2048,64]{0,1:T(8,128)(2,1)S(1)} %reshape.229, f32[2048]{0:T(1024)S(1)} %get-tuple-element.38, f32[2048]{0:T(1024)S(1)} %get-tuple-element.36, f32[2048,2048]{0,1:T(8,128)} %copy-done.1, bf16[2048,192]{0,1:T(8,128)(2,1)S(1)} %fusion.20), kind=kOutput, calls=%fused_computation.4 | convolution fusion | flops 557842432 | bytes 25706496 | tf_op jit(solution)/shard_map/dot_general | solution.py:56
  130.5 7.4 %all-to-all-start.6 = ((bf16[16,32,192]{2,1,0:T(8,128)(2,1)}), bf16[16,32,192]{2,1,0:T(8,128)(2,1)S(1)}, u32[]{:S(2)}, u32[]{:S(2)}) async-start(bf16[16,32,192]{2,1,0:T(8,128)(2,1)} %fusion.69), calls=%async_computation.6 | async-start | bytes 524288 | tf_op jit(solution)/shard_map/all_to_all | solution.py:62
  139.7 5.3 %all-to-all-done.6 = bf16[16,32,192]{2,1,0:T(8,128)(2,1)S(1)} async-done(((bf16[16,32,192]{2,1,0:T(8,128)(2,1)}), bf16[16,32,192]{2,1,0:T(8,128)(2,1)S(1)}, u32[]{:S(2)}, u32[]{:S(2)}) %all-to-all-start.6) | async-done | bytes 196640 | tf_op jit(solution)/shard_map/all_to_all | solution.py:62
  145.0 4.3 %all-to-all-start.1 = ((bf16[8,256,128]{2,1,0:T(8,128)(2,1)}), bf16[8,256,128]{2,1,0:T(8,128)(2,1)}, u32[]{:S(2)}, u32[]{:S(2)}) async-start(bf16[8,256,128]{2,1,0:T(8,128)(2,1)} %gather_fusion.1), calls=%async_computation.1 | async-start | bytes 1048576 | tf_op jit(solution)/shard_map/all_to_all | solution.py:62
  158.6 8.0 %all-to-all-done.1 = bf16[8,256,128]{2,1,0:T(8,128)(2,1)} async-done(((bf16[8,256,128]{2,1,0:T(8,128)(2,1)}), bf16[8,256,128]{2,1,0:T(8,128)(2,1)}, u32[]{:S(2)}, u32[]{:S(2)}) %all-to-all-start.1) | async-done | bytes 524320 | tf_op jit(solution)/shard_map/all_to_all | solution.py:62
  166.6 4.1 %all-to-all-start.2 = ((bf16[8,256,128]{2,1,0:T(8,128)(2,1)}), bf16[8,256,128]{2,1,0:T(8,128)(2,1)}, u32[]{:S(2)}, u32[]{:S(2)}) async-start(bf16[8,256,128]{2,1,0:T(8,128)(2,1)} %gather_fusion.3), calls=%async_computation.2 | async-start | bytes 1048576 | tf_op jit(solution)/shard_map/all_to_all | solution.py:62
  175.5 12.8 %all-to-all-done.2 = bf16[8,256,128]{2,1,0:T(8,128)(2,1)} async-done(((bf16[8,256,128]{2,1,0:T(8,128)(2,1)}), bf16[8,256,128]{2,1,0:T(8,128)(2,1)}, u32[]{:S(2)}, u32[]{:S(2)}) %all-to-all-start.2) | async-done | bytes 524320 | tf_op jit(solution)/shard_map/all_to_all | solution.py:62
  188.2 5.7 %all-to-all-start.3 = ((bf16[16,32,1024]{2,1,0:T(8,128)(2,1)}), bf16[16,32,1024]{2,1,0:T(8,128)(2,1)}, u32[]{:S(2)}, u32[]{:S(2)}) async-start(bf16[16,32,1024]{2,1,0:T(8,128)(2,1)} %fusion.8), calls=%async_computation.3 | async-start | bytes 2097152 | tf_op jit(solution)/shard_map/all_to_all | solution.py:62
  201.2 8.3 %all-to-all-done.3 = bf16[16,32,1024]{2,1,0:T(8,128)(2,1)} async-done(((bf16[16,32,1024]{2,1,0:T(8,128)(2,1)}), bf16[16,32,1024]{2,1,0:T(8,128)(2,1)}, u32[]{:S(2)}, u32[]{:S(2)}) %all-to-all-start.3) | async-done | bytes 1048608 | tf_op jit(solution)/shard_map/all_to_all | solution.py:62
  209.5 6.7 %all-to-all-start.4 = ((bf16[16,16,1024]{2,1,0:T(8,128)(2,1)}), bf16[16,16,1024]{2,1,0:T(8,128)(2,1)}, u32[]{:S(2)}, u32[]{:S(2)}) async-start(bf16[16,16,1024]{2,1,0:T(8,128)(2,1)} %fusion.38), calls=%async_computation.4 | async-start | bytes 1048576 | tf_op jit(solution)/shard_map/all_to_all | solution.py:62
  230.9 8.4 %all-to-all-done.5 = bf16[8,6,1024]{2,1,0:T(8,128)(2,1)S(1)} async-done(((bf16[8,6,1024]{2,1,0:T(8,128)(2,1)}), bf16[8,6,1024]{2,1,0:T(8,128)(2,1)S(1)}, u32[]{:S(2)}, u32[]{:S(2)}) %all-to-all-start.5) | async-done | bytes 98336 | tf_op jit(solution)/shard_map/all_to_all | solution.py:62
  240.8 4.0 %all-to-all-start.7 = ((bf16[8,48,256]{2,1,0:T(8,128)(2,1)}), bf16[8,48,256]{2,1,0:T(8,128)(2,1)}, u32[]{:S(2)}, u32[]{:S(2)}) async-start(bf16[8,48,256]{2,1,0:T(8,128)(2,1)} %broadcast_in_dim.5), calls=%async_computation.7 | async-start | bytes 393216 | tf_op jit(solution)/shard_map/all_to_all | solution.py:62
  248.5 6.1 %all-to-all-done.7 = bf16[8,48,256]{2,1,0:T(8,128)(2,1)} async-done(((bf16[8,48,256]{2,1,0:T(8,128)(2,1)}), bf16[8,48,256]{2,1,0:T(8,128)(2,1)}, u32[]{:S(2)}, u32[]{:S(2)}) %all-to-all-start.7) | async-done | bytes 196640 | tf_op jit(solution)/shard_map/all_to_all | solution.py:62
  (167 shorter events, 106.6 us)
Async XLA Ops:
  2.0 217.5 %copy-start.20 = (f32[256]{0:T(256)}, f32[256]{0:T(256)S(1)}, u32[]{:S(2)}) copy-start(f32[256]{0:T(256)S(1)} %add_rsqrt_fusion.2) | copy-start | bytes 3076
  4.0 30.4 %copy-start.5 = (bf16[256,1024]{1,0:T(8,128)(2,1)}, bf16[256,1024]{1,0:T(8,128)(2,1)S(1)}, u32[]{:S(2)}) copy-start(bf16[256,1024]{1,0:T(8,128)(2,1)S(1)} %get-tuple-element.13) | copy-start | bytes 1572868
  4.0 30.4 %collective-permute-start.4 = (bf16[256,1024]{1,0:T(8,128)(2,1)S(1)}, bf16[256,1024]{1,0:T(8,128)(2,1)S(1)}, u32[]{:S(2)}, u32[]{:S(2)}) collective-permute-start(bf16[256,1024]{1,0:T(8,128)(2,1)S(1)} %get-tuple-element.13), channel_id=1, source_target_pairs={{1,0},{2,1},{3,2},{4,3},{5,4},{6,5},{7,6},{0,7},{9,8},{10,9},{11,1... | collective-permute-start | bytes 1572872 | tf_op jit(solution)/shard_map/ppermute | solution.py:70
  9.9 24.6 %collective-permute-start = (bf16[256,1024]{1,0:T(8,128)(2,1)S(1)}, bf16[256,1024]{1,0:T(8,128)(2,1)}, u32[]{:S(2)}, u32[]{:S(2)}) collective-permute-start(bf16[256,1024]{1,0:T(8,128)(2,1)S(1)} %get-tuple-element.13), channel_id=1, source_target_pairs={{0,1},{1,2},{2,3},{3,4},{4,5},{5,6},{6,7},{7,0},{8,9},{9,10},{10,1... | collective-permute-start | bytes 1572872 | tf_op jit(solution)/shard_map/ppermute | solution.py:66
  12.4 17.7 %all-to-all-start = ((bf16[8,128,128]{1,2,0:T(8,128)(2,1)}), bf16[8,128,128]{1,2,0:T(8,128)(2,1)S(1)}, u32[]{:S(2)}, u32[]{:S(2)}) async-start(bf16[8,128,128]{1,2,0:T(8,128)(2,1)} %bitcast.3), calls=%async_computation | async-start | bytes 524288 | tf_op jit(solution)/shard_map/all_to_all | solution.py:62
  53.9 14.9 %collective-permute-start.5 = (bf16[256,1024]{1,0:T(8,128)(2,1)S(1)}, bf16[256,1024]{1,0:T(8,128)(2,1)S(1)}, u32[]{:S(2)}, u32[]{:S(2)}) collective-permute-start(bf16[256,1024]{1,0:T(8,128)(2,1)S(1)} %collective-permute-done.4), channel_id=1, source_target_pairs={{1,0},{2,1},{3,2},{4,3},{5,4},{6,5},{7,6},{0,7},{9,8},{10,9},{11,1... | collective-permute-start | bytes 1572872 | tf_op jit(solution)/shard_map/ppermute | solution.py:70
  54.0 16.6 %collective-permute-start.1 = (bf16[256,1024]{1,0:T(8,128)(2,1)}, bf16[256,1024]{1,0:T(8,128)(2,1)S(1)}, u32[]{:S(2)}, u32[]{:S(2)}) collective-permute-start(bf16[256,1024]{1,0:T(8,128)(2,1)} %collective-permute-done), channel_id=1, source_target_pairs={{0,1},{1,2},{2,3},{3,4},{4,5},{5,6},{6,7},{7,0},{8,9},{9,10},{10,1... | collective-permute-start | bytes 1572872 | tf_op jit(solution)/shard_map/ppermute | solution.py:66
  60.7 66.5 %collective-permute-start.8 = (bf16[2,128,1024]{2,1,0:T(8,128)(2,1)}, bf16[2,128,1024]{2,1,0:T(8,128)(2,1)}, u32[]{:S(2)}, u32[]{:S(2)}) collective-permute-start(bf16[2,128,1024]{2,1,0:T(8,128)(2,1)} %get-tuple-element.18), channel_id=1, source_target_pairs={{1,0},{2,1},{3,2},{4,3},{5,4},{6,5},{7,6},{0,7},{9,8},{10,9},{11,1... | collective-permute-start | bytes 1572872 | tf_op jit(solution)/shard_map/ppermute | solution.py:70
  62.0 65.2 %collective-permute-start.9 = (bf16[2,128,1024]{2,1,0:T(8,128)(2,1)}, bf16[2,128,1024]{2,1,0:T(8,128)(2,1)}, u32[]{:S(2)}, u32[]{:S(2)}) collective-permute-start(bf16[2,128,1024]{2,1,0:T(8,128)(2,1)} %get-tuple-element.19), channel_id=1, source_target_pairs={{0,1},{1,2},{2,3},{3,4},{4,5},{5,6},{6,7},{7,0},{8,9},{9,10},{10,1... | collective-permute-start | bytes 1572872 | tf_op jit(solution)/shard_map/ppermute | solution.py:66
  68.8 19.6 %collective-permute-start.6 = (bf16[256,1024]{1,0:T(8,128)(2,1)S(1)}, bf16[256,1024]{1,0:T(8,128)(2,1)S(1)}, u32[]{:S(2)}, u32[]{:S(2)}) collective-permute-start(bf16[256,1024]{1,0:T(8,128)(2,1)S(1)} %collective-permute-done.5), channel_id=1, source_target_pairs={{1,0},{2,1},{3,2},{4,3},{5,4},{6,5},{7,6},{0,7},{9,8},{10,9},{11,1... | collective-permute-start | bytes 1572872 | tf_op jit(solution)/shard_map/ppermute | solution.py:70
  70.6 19.2 %collective-permute-start.2 = (bf16[256,1024]{1,0:T(8,128)(2,1)S(1)}, bf16[256,1024]{1,0:T(8,128)(2,1)S(1)}, u32[]{:S(2)}, u32[]{:S(2)}) collective-permute-start(bf16[256,1024]{1,0:T(8,128)(2,1)S(1)} %collective-permute-done.1), channel_id=1, source_target_pairs={{0,1},{1,2},{2,3},{3,4},{4,5},{5,6},{6,7},{7,0},{8,9},{9,10},{10,1... | collective-permute-start | bytes 1572872 | tf_op jit(solution)/shard_map/ppermute | solution.py:66
  88.5 6.5 %collective-permute-start.7 = (bf16[128,1024]{1,0:T(8,128)(2,1)S(1)}, bf16[128,1024]{1,0:T(8,128)(2,1)S(1)}, u32[]{:S(2)}, u32[]{:S(2)}) collective-permute-start(bf16[128,1024]{1,0:T(8,128)(2,1)S(1)} %slice.79), channel_id=1, source_target_pairs={{1,0},{2,1},{3,2},{4,3},{5,4},{6,5},{7,6},{0,7},{9,8},{10,9},{11,1... | collective-permute-start | bytes 786440 | tf_op jit(solution)/shard_map/ppermute | solution.py:70
  89.8 7.7 %collective-permute-start.3 = (bf16[128,1024]{1,0:T(8,128)(2,1)S(1)}, bf16[128,1024]{1,0:T(8,128)(2,1)S(1)}, u32[]{:S(2)}, u32[]{:S(2)}) collective-permute-start(bf16[128,1024]{1,0:T(8,128)(2,1)S(1)} %slice.78), channel_id=1, source_target_pairs={{0,1},{1,2},{2,3},{3,4},{4,5},{5,6},{6,7},{7,0},{8,9},{9,10},{10,1... | collective-permute-start | bytes 786440 | tf_op jit(solution)/shard_map/ppermute | solution.py:66
  127.1 2.7 %collective-permute-start.12 = (bf16[16,32,192]{2,1,0:T(8,128)(2,1)S(1)}, bf16[16,32,192]{2,1,0:T(8,128)(2,1)S(1)}, u32[]{:S(2)}, u32[]{:S(2)}) collective-permute-start(bf16[16,32,192]{2,1,0:T(8,128)(2,1)S(1)} %dynamic-slice_bitcast_fusion.2), channel_id=1, source_target_pairs={{0,8},{8,0},{1,9},{9,1},{2,10},{10,2},{3,11},{11,3},{4,12},{12,4},... | collective-permute-start | bytes 589832 | tf_op jit(solution)/shard_map/ppermute | solution.py:79
  130.5 14.5 %all-to-all-start.6 = ((bf16[16,32,192]{2,1,0:T(8,128)(2,1)}), bf16[16,32,192]{2,1,0:T(8,128)(2,1)S(1)}, u32[]{:S(2)}, u32[]{:S(2)}) async-start(bf16[16,32,192]{2,1,0:T(8,128)(2,1)} %fusion.69), calls=%async_computation.6 | async-start | bytes 524288 | tf_op jit(solution)/shard_map/all_to_all | solution.py:62
  145.0 21.6 %all-to-all-start.1 = ((bf16[8,256,128]{2,1,0:T(8,128)(2,1)}), bf16[8,256,128]{2,1,0:T(8,128)(2,1)}, u32[]{:S(2)}, u32[]{:S(2)}) async-start(bf16[8,256,128]{2,1,0:T(8,128)(2,1)} %gather_fusion.1), calls=%async_computation.1 | async-start | bytes 1048576 | tf_op jit(solution)/shard_map/all_to_all | solution.py:62
  152.3 18.4 %collective-permute-start.10 = (bf16[16,32,1024]{2,1,0:T(8,128)(2,1)}, bf16[16,32,1024]{2,1,0:T(8,128)(2,1)}, u32[]{:S(2)}, u32[]{:S(2)}) collective-permute-start(bf16[16,32,1024]{2,1,0:T(8,128)(2,1)} %dynamic-slice_bitcast_fusion), channel_id=1, source_target_pairs={{0,8},{8,0},{1,9},{9,1},{2,10},{10,2},{3,11},{11,3},{4,12},{12,4},... | collective-permute-start | bytes 3145736 | tf_op jit(solution)/shard_map/ppermute | solution.py:79
  166.6 21.6 %all-to-all-start.2 = ((bf16[8,256,128]{2,1,0:T(8,128)(2,1)}), bf16[8,256,128]{2,1,0:T(8,128)(2,1)}, u32[]{:S(2)}, u32[]{:S(2)}) async-start(bf16[8,256,128]{2,1,0:T(8,128)(2,1)} %gather_fusion.3), calls=%async_computation.2 | async-start | bytes 1048576 | tf_op jit(solution)/shard_map/all_to_all | solution.py:62
  188.2 21.3 %all-to-all-start.3 = ((bf16[16,32,1024]{2,1,0:T(8,128)(2,1)}), bf16[16,32,1024]{2,1,0:T(8,128)(2,1)}, u32[]{:S(2)}, u32[]{:S(2)}) async-start(bf16[16,32,1024]{2,1,0:T(8,128)(2,1)} %fusion.8), calls=%async_computation.3 | async-start | bytes 2097152 | tf_op jit(solution)/shard_map/all_to_all | solution.py:62
  196.3 2.8 %collective-permute-start.11 = (bf16[16,16,1024]{2,1,0:T(8,128)(2,1)}, bf16[16,16,1024]{2,1,0:T(8,128)(2,1)S(1)}, u32[]{:S(2)}, u32[]{:S(2)}) collective-permute-start(bf16[16,16,1024]{2,1,0:T(8,128)(2,1)} %dynamic-slice_bitcast_fusion.1), channel_id=1, source_target_pairs={{0,8},{8,0},{1,9},{9,1},{2,10},{10,2},{3,11},{11,3},{4,12},{12,4},... | collective-permute-start | bytes 1572872 | tf_op jit(solution)/shard_map/ppermute | solution.py:79
  209.5 14.8 %all-to-all-start.4 = ((bf16[16,16,1024]{2,1,0:T(8,128)(2,1)}), bf16[16,16,1024]{2,1,0:T(8,128)(2,1)}, u32[]{:S(2)}, u32[]{:S(2)}) async-start(bf16[16,16,1024]{2,1,0:T(8,128)(2,1)} %fusion.38), calls=%async_computation.4 | async-start | bytes 1048576 | tf_op jit(solution)/shard_map/all_to_all | solution.py:62
  221.3 25.9 %copy-start.7 = (f32[256,1024]{1,0:T(8,128)S(1)}, f32[256,1024]{1,0:T(8,128)}, u32[]{:S(2)}) copy-start(f32[256,1024]{1,0:T(8,128)} %get-tuple-element.21) | copy-start | bytes 3145732
  227.0 12.4 %all-to-all-start.5 = ((bf16[8,6,1024]{2,1,0:T(8,128)(2,1)}), bf16[8,6,1024]{2,1,0:T(8,128)(2,1)S(1)}, u32[]{:S(2)}, u32[]{:S(2)}) async-start(bf16[8,6,1024]{2,1,0:T(8,128)(2,1)} %convert_element_type.228), calls=%async_computation.5 | async-start | bytes 262144 | tf_op jit(solution)/shard_map/all_to_all | solution.py:62
  240.8 13.8 %all-to-all-start.7 = ((bf16[8,48,256]{2,1,0:T(8,128)(2,1)}), bf16[8,48,256]{2,1,0:T(8,128)(2,1)}, u32[]{:S(2)}, u32[]{:S(2)}) async-start(bf16[8,48,256]{2,1,0:T(8,128)(2,1)} %broadcast_in_dim.5), calls=%async_computation.7 | async-start | bytes 393216 | tf_op jit(solution)/shard_map/all_to_all | solution.py:62
  (21 other events, 218.4 us)

commit v2 on v1

v2 whole, which is shorter than its diff:
```python
import jax
import jax.numpy as jnp
from jax import lax
from jax.experimental import pallas as pl
from jax.experimental.pallas import tpu as pltpu
from jax.sharding import Mesh
from jax.sharding import PartitionSpec as P

HEAD_DIM = 64
BLOCK = 128
N_SEQ = 8
N_XY = 16
CHUNK = 256

exponent_divisor = 32.0
epsilon = 1e-06


def unit_rows(block):
    wide = block.astype(jnp.float32)
    factor = lax.rsqrt(jnp.mean(wide * wide, axis=-1, keepdims=True) + epsilon)
    return (wide, factor)


def matmul(left, right):
    return jnp.dot(left, right, preferred_element_type=jnp.float32)


def forward_kernel(*refs):
    z_ref = refs[0]
    chunks = refs[1:9]
    w_ref, dh_ref = refs[9:11]
    att_ref, rows_ref, turned_ref, raw_ref, stats_ref = refs[11:16]
    dv_sum = refs[16]
    z = z_ref[0]
    scale = exponent_divisor / HEAD_DIM
    half = CHUNK // 2
    for j in range(N_SEQ):
        proj = matmul(chunks[j][...], w_ref[...]).astype(jnp.bfloat16)
        wide = proj.astype(jnp.float32)
        query, keyrow, valrow = (wide[:, i * HEAD_DIM : (i + 1) * HEAD_DIM] for i in range(3))
        _, q_factor = unit_rows(query)
        _, k_factor = unit_rows(keyrow)
        q_unit = query * q_factor
        k_unit = keyrow * k_factor
        folded = dh_ref[lax.rem(z - j + N_SEQ, N_SEQ)]
        d_head = jnp.concatenate([folded[:, :HEAD_DIM], folded[:, HEAD_DIM:]], axis=0)
        rows_ref[0, j] = q_unit.astype(jnp.bfloat16)
        rows_ref[1, j] = k_unit.astype(jnp.bfloat16)
        rows_ref[2, j] = valrow.astype(jnp.bfloat16)
        rows_ref[3, j] = d_head
        raw_ref[0, j] = jnp.concatenate([keyrow, jnp.broadcast_to(k_factor, keyrow.shape)], axis=1)
        first = jnp.concatenate([q_unit, d_head.astype(jnp.float32)], axis=1).T
        second = jnp.concatenate([k_unit, valrow], axis=1).T
        turned_ref[0, j] = first[:HEAD_DIM].astype(jnp.bfloat16)
        turned_ref[1, j] = first[HEAD_DIM:].astype(jnp.bfloat16)
        turned_ref[2, j] = second[:HEAD_DIM].astype(jnp.bfloat16)
        turned_ref[3, j] = second[HEAD_DIM:].astype(jnp.bfloat16)
        raw_ref[1, j] = jnp.concatenate([query, jnp.broadcast_to(q_factor, query.shape)], axis=1)
    dv_sum[...] = jnp.zeros_like(dv_sum)

    def step(i, carry):
        keys = rows_ref[1].reshape(N_SEQ * CHUNK, HEAD_DIM)
        scores = matmul(keys, turned_ref[0, i]) * scale
        exps = jnp.exp(scores)
        inverse = 1.0 / jnp.sum(exps, axis=0, keepdims=True)
        prob_low = (exps * inverse).astype(jnp.bfloat16)
        out = jnp.zeros((HEAD_DIM, CHUNK), jnp.float32)
        for j in range(N_SEQ):
            out += matmul(turned_ref[3, j], prob_low[j * CHUNK : (j + 1) * CHUNK])
        dv_sum[...] += matmul(prob_low, rows_ref[3, i])
        out = out.astype(jnp.bfloat16).astype(jnp.float32)
        d_head = turned_ref[1, i].astype(jnp.float32)
        stats_ref[i, 0:1] = inverse
        stats_ref[i, 1:2] = jnp.sum(out * d_head, axis=0, keepdims=True)
        both = jnp.concatenate([out, out], axis=0).T
        att_ref[lax.rem(z - i + N_SEQ, N_SEQ)] = both.astype(jnp.bfloat16)
        return carry

    lax.fori_loop(0, N_SEQ, step, 0)
    for j in range(N_SEQ):
        place = lax.rem(z - j + N_SEQ, N_SEQ)
        att_ref[place, :, HEAD_DIM:] = dv_sum[j * CHUNK : (j + 1) * CHUNK].astype(jnp.bfloat16)


def backward_kernel(*refs):
    place_ref = refs[0]
    chunks = refs[1:9]
    att_ref, rows_ref, turned_ref, raw_ref, stats_ref = refs[9:14]
    dqk_ref, keep_ref, give_ref = refs[14:17]
    dk_sum, dqt, grad_t, grad = refs[17:21]
    z = place_ref[0]
    core = place_ref[1]
    scale = exponent_divisor / HEAD_DIM
    dk_sum[...] = jnp.zeros_like(dk_sum)

    def step(i, carry):
        keys = rows_ref[1].reshape(N_SEQ * CHUNK, HEAD_DIM)
        vals = rows_ref[2].reshape(N_SEQ * CHUNK, HEAD_DIM)
        scores = matmul(keys, turned_ref[0, i]) * scale
        prob = jnp.exp(scores) * stats_ref[i, 0:1]
        d_prob = matmul(vals, turned_ref[1, i])
        d_scores = (prob * (d_prob - stats_ref[i, 1:2])).astype(jnp.bfloat16)
        d_qunit = jnp.zeros((HEAD_DIM, CHUNK), jnp.float32)
        for j in range(N_SEQ):
            d_qunit += matmul(turned_ref[2, j], d_scores[j * CHUNK : (j + 1) * CHUNK])
        dk_sum[...] += matmul(d_scores, rows_ref[0, i])
        dqt[i] = d_qunit * scale
        return carry

    lax.fori_loop(0, N_SEQ, step, 0)
    for j in range(N_SEQ):
        place = lax.rem(z - j + N_SEQ, N_SEQ)
        d_qunit = jnp.concatenate([dqt[j], dqt[j]], axis=0).T[:, :HEAD_DIM]
        d_kunit = dk_sum[j * CHUNK : (j + 1) * CHUNK] * scale
        parts = []
        for raw, d_unit in ((raw_ref[1, j], d_qunit), (raw_ref[0, j], d_kunit)):
            wide = raw[:, :HEAD_DIM]
            factor = raw[:, HEAD_DIM:]
            mean = jnp.mean(d_unit * wide, axis=-1, keepdims=True)
            parts.append(factor * d_unit - factor * factor * factor * wide * mean)
        both = jnp.concatenate(parts, axis=1)
        dqk_ref[place] = both.astype(jnp.bfloat16)
        d_val = att_ref[place].astype(jnp.float32)
        d_val = jnp.concatenate([d_val[:, HEAD_DIM:], jnp.zeros_like(d_val[:, HEAD_DIM:])], axis=1)
        stacked = jnp.concatenate([both.T, d_val.T], axis=0).astype(jnp.bfloat16)
        term = matmul(stacked, chunks[j][...])
        if j == 0:
            grad_t[...] = term
        else:
            grad_t[...] += term
    grad[...] = grad_t[...].T
    rows = grad.shape[0] // (2 * N_XY)
    for i in range(N_XY):
        keep_ref[i] = grad[pl.ds((2 * i + core) * rows, rows), :].astype(jnp.bfloat16)
        give_ref[i] = grad[pl.ds((2 * i + 1 - core) * rows, rows), :].astype(jnp.bfloat16)


def in_vmem(count):
    return [pl.BlockSpec(memory_space=pltpu.VMEM)] * count


def attend_forward(z, chunks, w_head, d_heads):
    nodes = N_SEQ * CHUNK
    flops = 2 * nodes * (chunks[0].shape[1] * 3 * HEAD_DIM + 3 * nodes * HEAD_DIM)
    return pl.pallas_call(
        forward_kernel,
        out_shape=(
            jax.ShapeDtypeStruct((N_SEQ, CHUNK, 2 * HEAD_DIM), jnp.bfloat16),
            jax.ShapeDtypeStruct((4, N_SEQ, CHUNK, HEAD_DIM), jnp.bfloat16),
            jax.ShapeDtypeStruct((4, N_SEQ, HEAD_DIM, CHUNK), jnp.bfloat16),
            jax.ShapeDtypeStruct((2, N_SEQ, CHUNK, 2 * HEAD_DIM), jnp.float32),
            jax.ShapeDtypeStruct((N_SEQ, 8, CHUNK), jnp.float32),
        ),
        in_specs=[pl.BlockSpec(memory_space=pltpu.SMEM)] + in_vmem(10),
        out_specs=tuple(in_vmem(5)),
        scratch_shapes=[pltpu.VMEM((nodes, HEAD_DIM), jnp.float32)],
        compiler_params=pltpu.CompilerParams(vmem_limit_bytes=48 * 1024 * 1024),
        cost_estimate=pl.CostEstimate(
            flops=4 * flops, bytes_accessed=12 * 1024 * 1024, transcendentals=nodes * nodes
        ),
        name="attend_forward",
    )(z, *chunks, w_head, d_heads)


def attend_backward(place, chunks, att, saved):
    nodes = N_SEQ * CHUNK
    width = chunks[0].shape[1]
    flops = 2 * nodes * (width * 3 * HEAD_DIM + 4 * nodes * HEAD_DIM)
    part = jax.ShapeDtypeStruct((N_XY, width // (2 * N_XY), 4 * HEAD_DIM), jnp.bfloat16)
    return pl.pallas_call(
        backward_kernel,
        out_shape=(jax.ShapeDtypeStruct((N_SEQ, CHUNK, 2 * HEAD_DIM), jnp.bfloat16), part, part),
        in_specs=[pl.BlockSpec(memory_space=pltpu.SMEM)] + in_vmem(13),
        out_specs=tuple(in_vmem(3)),
        scratch_shapes=[
            pltpu.VMEM((nodes, HEAD_DIM), jnp.float32),
            pltpu.VMEM((N_SEQ, HEAD_DIM, CHUNK), jnp.float32),
            pltpu.VMEM((4 * HEAD_DIM, width), jnp.float32),
            pltpu.VMEM((width, 4 * HEAD_DIM), jnp.float32),
        ],
        compiler_params=pltpu.CompilerParams(vmem_limit_bytes=48 * 1024 * 1024),
        cost_estimate=pl.CostEstimate(
            flops=4 * flops, bytes_accessed=12 * 1024 * 1024, transcendentals=nodes * nodes
        ),
        name="attend_backward",
    )(place, *chunks, att, *saved)


def after(value, *others):
    return lax.optimization_barrier((value,) + others)[0]


def contract_rows(left, right):
    return lax.dot_general(
        left, right, (((0,), (0,)), ((), ())), preferred_element_type=jnp.float32
    )


def contract_cols(left, right):
    return lax.dot_general(
        left, right, (((1,), (1,)), ((), ())), preferred_element_type=jnp.float32
    )


def exchange(array, axis):
    return lax.all_to_all(array, axis, split_axis=0, concat_axis=0, tiled=True)


def up(array):
    return lax.ppermute(array, "z", [(i, (i + 1) % N_SEQ) for i in range(N_SEQ)])


def down(array):
    return lax.ppermute(array, "z", [((i + 1) % N_SEQ, i) for i in range(N_SEQ)])


def halves(partial):
    rows, width = partial.shape
    core = lax.axis_index("c")
    parts = partial.astype(jnp.bfloat16).reshape(N_XY, 2, rows // (2 * N_XY), width)
    keep = lax.dynamic_index_in_dim(parts, core, 1, keepdims=False)
    give = lax.dynamic_index_in_dim(parts, 1 - core, 1, keepdims=False)
    return keep, give


def sum_over_cores(keep, give):
    got = lax.ppermute(give, "c", [(0, 1), (1, 0)])
    return (keep.astype(jnp.float32) + got.astype(jnp.float32)).astype(jnp.bfloat16)


def sum_over_chips(pair):
    return jnp.sum(exchange(pair, ("x", "y")).astype(jnp.float32), axis=0)


def on_device(
    features, out_grad, norm_gain, w_qkv, w_out, w_msg, block_ids, block_counts, edge_tiles
):
    node_rows, width = features.shape
    hd = w_out.shape[0]
    z = lax.axis_index("z")
    core = lax.axis_index("c")
    place = jnp.stack([z, core]).astype(jnp.int32)
    feat_wide = features.astype(jnp.float32)
    inv_rms = lax.rsqrt(jnp.mean(feat_wide * feat_wide, axis=-1, keepdims=True) + epsilon)
    x_hat = feat_wide * inv_rms
    normed = (x_hat * norm_gain).astype(jnp.bfloat16)

    a1, b1 = up(normed), down(normed)
    a2, b2 = up(a1), down(b1)
    a3, b3 = up(a2), down(b2)
    half = node_rows // 2
    c4 = jnp.concatenate([up(a3[:half]), down(b3[half:])], axis=0)
    chunks = [normed, a1, a2, a3, c4, b3, b2, b1]

    d_out = contract_cols(out_grad, w_out).astype(jnp.bfloat16)
    d_out = d_out.reshape(2, half, N_SEQ, HEAD_DIM).transpose(2, 1, 0, 3).reshape(N_SEQ, half, 2 * HEAD_DIM)
    d_heads = exchange(d_out, "z")
    w_head = lax.dynamic_index_in_dim(w_qkv.reshape(width, 3, N_SEQ, HEAD_DIM), z, 2, keepdims=False)
    w_head = w_head.reshape(width, 3 * HEAD_DIM)

    wide = jnp.concatenate([after(a1, a2, b2), normed, b1], axis=0)
    blocks_here = node_rows // BLOCK
    wide_msg = jnp.dot(wide, w_msg, preferred_element_type=jnp.float32).astype(jnp.bfloat16)
    local_ids = block_ids - (z - 1) * blocks_here
    source = wide_msg.reshape(3 * blocks_here, BLOCK, width)[local_ids]
    slots = block_ids.shape[1]
    live_mask = (jnp.arange(slots, dtype=jnp.int32)[None, :] < block_counts[:, None]).astype(jnp.bfloat16)
    live = edge_tiles * live_mask[:, :, None, None]
    agg = jnp.einsum("bsij,bsjd->bid", live, source, preferred_element_type=jnp.float32).reshape(
        node_rows, width
    )
    grad_wide = out_grad.astype(jnp.float32)
    sigma = jax.nn.sigmoid(agg)
    d_agg = (grad_wide * sigma * (1.0 + agg * (1.0 - sigma))).astype(jnp.bfloat16)
    contrib = jnp.einsum(
        "bsij,bid->bsjd",
        live,
        d_agg.reshape(blocks_here, BLOCK, width),
        preferred_element_type=jnp.float32,
    )
    tally = (
        local_ids[:, :, None] == jnp.arange(3 * blocks_here, dtype=jnp.int32)[None, None, :]
    ).astype(jnp.float32)
    landed = jnp.einsum("bsk,bsjd->kjd", tally, contrib, precision=lax.Precision.HIGHEST)
    from_above = down(landed[:blocks_here].astype(jnp.bfloat16)).astype(jnp.float32)
    from_below = up(landed[2 * blocks_here :].astype(jnp.bfloat16)).astype(jnp.float32)
    d_msg = (
        (landed[blocks_here : 2 * blocks_here] + from_above + from_below)
        .reshape(node_rows, width)
        .astype(jnp.bfloat16)
    )
    sum_msg = sum_over_chips(sum_over_cores(*halves(contract_rows(normed, d_msg))))
    rows_msg = sum_msg.shape[0]
    cut_msg = sum_msg.astype(jnp.bfloat16).reshape(rows_msg, N_SEQ, width // N_SEQ).transpose(1, 0, 2)
    share_msg = jnp.sum(exchange(cut_msg, "z").astype(jnp.float32), axis=0).astype(jnp.bfloat16)

    att, *saved = attend_forward(place, chunks, w_head, d_heads)
    att_home = exchange(att, "z")
    d_heads_qk, keep, give = attend_backward(place, chunks, att, saved)

    out_rows = att_home[:, :, :HEAD_DIM].transpose(1, 0, 2).reshape(node_rows, hd)
    dv_rows = att_home[:, :, HEAD_DIM:].transpose(1, 0, 2).reshape(node_rows, hd)
    attn_part = jnp.dot(out_rows, w_out, preferred_element_type=jnp.float32)
    block_result_array = (feat_wide + attn_part + agg * sigma).astype(jnp.bfloat16)
    pair_out = sum_over_cores(*halves(contract_rows(out_rows, out_grad)))
    rows_out = pair_out.shape[1]

    pair_head = sum_over_cores(keep, give)
    lanes = pair_head.shape[2]
    pair_out = pair_out.reshape(N_XY, rows_out, width // lanes, lanes).transpose(0, 2, 1, 3)
    pair = jnp.concatenate([pair_head, pair_out.reshape(N_XY, -1, lanes)], axis=1)
    both = sum_over_chips(pair)
    sum_head = both[:rows_msg]
    sum_out = both[rows_msg:]

    dqk_home = exchange(d_heads_qk, "z")
    dq_rows = dqk_home[:, :, :HEAD_DIM].transpose(1, 0, 2).reshape(node_rows, hd)
    dk_rows = dqk_home[:, :, HEAD_DIM:].transpose(1, 0, 2).reshape(node_rows, hd)
    d_proj = jnp.concatenate([dq_rows, dk_rows, dv_rows], axis=1)
    d_norm = contract_cols(d_proj, w_qkv) + contract_cols(d_msg, w_msg)
    scaled = d_norm * norm_gain
    d_feat = inv_rms * (scaled - x_hat * jnp.mean(scaled * x_hat, axis=-1, keepdims=True))
    grad_input = (grad_wide + d_feat).astype(jnp.bfloat16)

    mine = jnp.concatenate(
        [sum_head[:, :BLOCK], sum_head[:, BLOCK:], sum_out[:, :BLOCK], sum_out[:, BLOCK:]], axis=0
    ).astype(jnp.bfloat16)
    mine = jnp.concatenate([mine, share_msg], axis=0)
    every = exchange(jnp.broadcast_to(mine[None], (N_SEQ,) + mine.shape), "z")
    nodes = N_SEQ * node_rows
    first_block = every[:, :rows_msg]
    heads = jnp.stack(
        [first_block[:, :, :HEAD_DIM], first_block[:, :, HEAD_DIM:], every[:, rows_msg : 2 * rows_msg, :HEAD_DIM]]
    )
    grad_qkv = heads.transpose(2, 0, 1, 3).reshape(rows_msg, 3 * hd).astype(jnp.float32) / nodes
    count = sum_out.shape[0]
    tall = jnp.sum(every[:, 2 * rows_msg : 2 * rows_msg + 2 * count].astype(jnp.float32), axis=0) / nodes
    tall = tall.reshape(2, width // lanes, rows_out, BLOCK).transpose(2, 1, 0, 3)
    grad_out = tall.reshape(rows_out, width)
    grad_msg = every[:, 2 * rows_msg + 2 * count :].transpose(1, 0, 2).reshape(rows_msg, width).astype(jnp.float32)
    grad_msg = grad_msg / nodes

    first = ((lax.axis_index("x") * 4 + lax.axis_index("y")) * 2 + core) * rows_msg
    w_rows = lax.dynamic_slice_in_dim(w_qkv, first, rows_msg, 0).astype(jnp.float32)
    m_rows = lax.dynamic_slice_in_dim(w_msg, first, rows_msg, 0).astype(jnp.float32)
    gain_rows = lax.dynamic_slice_in_dim(norm_gain, first, rows_msg, 0)
    grad_gain = (
        jnp.sum(w_rows * grad_qkv, axis=1) + jnp.sum(m_rows * grad_msg, axis=1)
    ) / gain_rows
    return block_result_array, grad_input, grad_gain, grad_qkv, grad_out, grad_msg


def solution(mesh):
    fine = Mesh(mesh.devices.reshape(4, 4, 2, N_SEQ), ("x", "y", "c", "z"))
    dp = ("x", "y", "c")
    rows = ("x", "y", "c", "z")
    return jax.shard_map(
        on_device,
        mesh=fine,
        in_specs=(
            P(rows, None),
            P(rows, None),
            P(),
            P(),
            P(),
            P(),
            P(rows, None),
            P(rows),
            P(rows, None, None, None),
        ),
        out_specs=(
            P(rows, None),
            P(rows, None),
            P(dp),
            P(dp, None),
            P(dp, None),
            P(dp, None),
        ),
        check_vma=False,
    )
```

time: 266 us -> 256 us (0.962)
  Pallas kernels: 0 us -> 38.6 us
  matrix products: 49 us -> 22.1 us
  waiting for transfers between devices: 83.2 us -> 70.8 us
  other arithmetic: 35.3 us -> 26.2 us
    pallas_call x0 -> x2, Pallas kernels: none -> 38.6 us  [the longest x1 19.7 us: attend_forward(): pl.pallas_call(forward_kernel, out_shape=(jax.ShapeDtypeStruct((N_SEQ, CH...]
    ppermute x5, waiting for transfers between devices: 3.21 us -> 22.9 us  [up(): lax.ppermute(array, 'z', [(i, (i + 1) % N_SEQ) for i in range(N_SEQ)])]
    ppermute x5, waiting for transfers between devices: 24.1 us -> 6.25 us  [down(): lax.ppermute(array, 'z', [((i + 1) % N_SEQ, i) for i in range(N_SEQ)])]
    all_to_all x8 -> x7, waiting for transfers between devices: 55.9 us -> 39.9 us  [exchange(): return lax.all_to_all(array, axis, split_axis=0, concat_axis=0, tiled=True)]
    dot_general x5 -> x3, matrix products: 16.9 us -> 5.49 us  [contract_cols(): lax.dot_general(left, right, (((1,), (1,)), ((), ())), preferred_element_...]
    dot_general x10 -> x0, matrix products: 7.75 us -> none  [the longest x8 3.7 us: on_device(): jnp.dot(c, w_head, preferred_element_type=jnp.float32).astype(jnp.bfloat16)]
    transpose x1 -> x9, local copies, waits for them, and re-layouts: 1.92 us -> 9.5 us  [the longest x2 4.2 us: on_device(): att_home[:, :, HEAD_DIM:].transpose(1, 0, 2).reshape(node_rows, hd)]
    dot_general x5 -> x2, matrix products: 8.69 us -> 1.21 us  [contract_rows(): lax.dot_general(left, right, (((0,), (0,)), ((), ())), preferred_element_...]
  transfers between devices with their start and end apart: 21 -> 20, of which waited for: 14 -> 10; matrix products, arithmetic and copies ran while one was open for 32% -> 18% of each run, Pallas kernels for 0% -> 15%
where the time goes in v2:
time: 256 us; the launch traced here: 251 us
  waiting for transfers between devices  70.8 us (28%)
  starting transfers between devices  56.4 us (22%)
  Pallas kernels  38.6 us (15%)
  local copies, waits for them, and re-layouts  35.4 us (14%)
  other arithmetic  26.2 us (10%)
  matrix products  22.1 us (9%)
    all_to_all x7, waiting for transfers between devices, exchange(): return lax.all_to_all(array, axis, split_axis=0, concat_axis=0, tiled=True)  39.9 us
    all_to_all x7, starting transfers between devices, exchange(): return lax.all_to_all(array, axis, split_axis=0, concat_axis=0, tiled=True)  37.7 us
    ppermute x5, waiting for transfers between devices, up(): lax.ppermute(array, 'z', [(i, (i + 1) % N_SEQ) for i in range(N_SEQ)])  22.9 us
    pallas_call x1, Pallas kernels, attend_forward(): pl.pallas_call(forward_kernel, out_shape=(jax.ShapeDtypeStruct((N_SEQ, CH...  19.7 us
    pallas_call x1, Pallas kernels, attend_backward(): pl.pallas_call(backward_kernel, out_shape=(jax.ShapeDtypeStruct((N_SEQ, C...  19 us
    ppermute x5, starting transfers between devices, down(): lax.ppermute(array, 'z', [((i + 1) % N_SEQ, i) for i in range(N_SEQ)])  14.2 us
    unnamed x55, local copies, waits for them, and re-layouts  11.7 us
    dot_general x1, matrix products, on_device(): jnp.einsum('bsk,bsjd->kjd', tally, contrib, precision=lax.Precision.HIGHEST)  6.64 us
  transfers between devices with their start and end apart: 20, of which 10 were waited for; matrix products, arithmetic and copies ran while one was open for 18% of the time, Pallas kernels for 15%

profile of v2, /device:TPU:6, one launch (start us, length us, event | category | flops | bytes accessed | tf_op | source)
XLA Modules:
  0.0 250.9 jit_solution(11914430649377879042)
XLA Ops:
  5.2 4.0 %collective-permute-start.4 = (bf16[256,1024]{1,0:T(8,128)(2,1)S(1)}, bf16[256,1024]{1,0:T(8,128)(2,1)S(1)}, u32[]{:S(2)}, u32[]{:S(2)}) collective-permute-start(bf16[256,1024]{1,0:T(8,128)(2,1)S(1)} %fusion.20.refs_1_), channel_id=1, source_target_pairs={{1,0},{2,1},{3,2},{4,3},{5,4},{6,5},{7,6},{0,7},{9,8},{10,9},{11,1... | collective-permute-start | bytes 1572872 | tf_op jit(solution)/shard_map/ppermute | solution.py:215
  9.2 11.8 %collective-permute-done.refs_2_ = bf16[256,1024]{1,0:T(8,128)(2,1)S(1)} collective-permute-done((bf16[256,1024]{1,0:T(8,128)(2,1)S(1)}, bf16[256,1024]{1,0:T(8,128)(2,1)S(1)}, u32[]{:S(2)}, u32[]{:S(2)}) %collective-permute-start) | collective-permute-done | bytes 524320 | tf_op jit(solution)/shard_map/ppermute | solution.py:211
  21.1 3.4 %collective-permute-start.5 = (bf16[256,1024]{1,0:T(8,128)(2,1)S(1)}, bf16[256,1024]{1,0:T(8,128)(2,1)}, u32[]{:S(2)}, u32[]{:S(2)}) collective-permute-start(bf16[256,1024]{1,0:T(8,128)(2,1)S(1)} %collective-permute-done.4.refs_8_), channel_id=1, source_target_pairs={{1,0},{2,1},{3,2},{4,3},{5,4},{6,5},{7,6},{0,7},{9,8},{10,9},{11,1... | collective-permute-start | bytes 1572872 | tf_op jit(solution)/shard_map/ppermute | solution.py:215
  26.0 9.5 %collective-permute-done.1.refs_3_ = bf16[256,1024]{1,0:T(8,128)(2,1)} collective-permute-done((bf16[256,1024]{1,0:T(8,128)(2,1)S(1)}, bf16[256,1024]{1,0:T(8,128)(2,1)}, u32[]{:S(2)}, u32[]{:S(2)}) %collective-permute-start.1) | collective-permute-done | bytes 524320 | tf_op jit(solution)/shard_map/ppermute | solution.py:211
  35.5 4.5 %convolution_convert_fusion.1 = bf16[768,1024]{1,0:T(8,128)(2,1)} fusion(bf16[1024,1024]{1,0:T(8,128)(2,1)} %param.14, bf16[256,1024]{1,0:T(8,128)(2,1)S(1)} %collective-permute-done.4.refs_8_, bf16[256,1024]{1,0:T(8,128)(2,1)S(1)} %fusion.20.refs_1_, bf16[256,1024]{1,0:T(8,128)(2,1)S(1)} %collective-permute-done.refs_2_), kind=kOutput, calls=%fused_computation.7 | convolution fusion | flops 1616117760 | bytes 5242880 | tf_op jit(solution)/shard_map/dot_general | solution.py:264
  40.0 3.5 %gather_fusion = bf16[8,128,1024]{2,1,0:T(8,128)(2,1)} fusion(bf16[6,128,1024]{2,1,0:T(8,128)(2,1)} %bitcast.117, s32[1024]{0:T(1024)S(1)} %pad_clamp_fusion), kind=kCustom, calls=%fused_computation | custom fusion | bytes 4194336 | tf_op jit(solution)/shard_map/gather | solution.py:266
  48.0 6.6 %fusion.2 = f32[6,128,1024]{2,0,1:T(8,128)S(1)} fusion(f32[2,4,128,1024]{3,2,1,0:T(8,128)S(1)} %fusion.38, s32[2,4]{1,0:T(2,128)S(1)} %get-tuple-element.29), kind=kOutput, calls=%fused_computation.3 | convolution fusion | flops 75497520 | bytes 7340064 | tf_op jit(solution)/shard_map/bsk,bsjd->kjd/dot_general | solution.py:285
  54.6 3.5 %fusion.49 = (bf16[6,128,1024]{2,1,0:T(8,128)(2,1)S(1)}, f32[6,128,1024]{2,1,0:T(8,128)}) fusion(f32[6,128,1024]{2,0,1:T(8,128)S(1)} %fusion.2), kind=kLoop, calls=%fused_computation.98 | loop fusion | flops 786432 | bytes 7864320 | tf_op jit(solution)/shard_map/convert.13
  59.2 3.6 %collective-permute-start.6 = (bf16[256,1024]{1,0:T(8,128)(2,1)}, bf16[256,1024]{1,0:T(8,128)(2,1)S(1)}, u32[]{:S(2)}, u32[]{:S(2)}) collective-permute-start(bf16[256,1024]{1,0:T(8,128)(2,1)} %collective-permute-done.5.refs_7_), channel_id=1, source_target_pairs={{1,0},{2,1},{3,2},{4,3},{5,4},{6,5},{7,6},{0,7},{9,8},{10,9},{11,1... | collective-permute-start | bytes 1572872 | tf_op jit(solution)/shard_map/ppermute | solution.py:215
  66.5 5.7 %all-to-all-start = ((bf16[8,128,128]{2,1,0:T(8,128)(2,1)}), bf16[8,128,128]{2,1,0:T(8,128)(2,1)S(1)}, u32[]{:S(2)}, u32[]{:S(2)}) async-start(bf16[8,128,128]{2,1,0:T(8,128)(2,1)} %copy.81), calls=%async_computation | async-start | bytes 524288 | tf_op jit(solution)/shard_map/all_to_all | solution.py:207
  72.2 4.7 %copy.78 = bf16[1024,1536]{0,1:T(8,128)(2,1)} copy(bf16[1024,1536]{1,0:T(8,128)(2,1)} %param.12) | data formatting | bytes 6291456 | tf_op args[3]
  83.3 5.5 %collective-permute-done.8 = bf16[2,128,1024]{2,1,0:T(8,128)(2,1)} collective-permute-done((bf16[2,128,1024]{2,1,0:T(8,128)(2,1)}, bf16[2,128,1024]{2,1,0:T(8,128)(2,1)}, u32[]{:S(2)}, u32[]{:S(2)}) %collective-permute-start.8) | collective-permute-done | bytes 524320 | tf_op jit(solution)/shard_map/ppermute | solution.py:215
  98.9 19.7 %attend_forward.1 = (bf16[8,256,128]{2,1,0:T(8,128)(2,1)}, bf16[4,8,256,64]{3,2,1,0:T(8,128)(2,1)}, bf16[4,8,64,256]{3,2,1,0:T(8,128)(2,1)}, f32[2,8,256,128]{3,2,1,0:T(8,128)}, f32[8,8,256]{2,1,0:T(8,128)S(1)}) custom-call(s32[2]{0:T(128)S(1)} %pad_add_fusion.refs_0_, bf16[256,1024]{1,0:T(8,128)(2,1)S(1)} %fusion.20.refs_1_, ...), custom_call_target="tpu_custom_call" | custom-call | flops 9663676416 | bytes 12582912 | tf_op jit(solution)/shard_map/attend_forward/pallas_call | solution.py:146
  118.5 5.9 %all-to-all-start.1 = ((bf16[8,256,128]{2,1,0:T(8,128)(2,1)}), bf16[8,256,128]{2,1,0:T(8,128)(2,1)}, u32[]{:S(2)}, u32[]{:S(2)}) async-start(bf16[8,256,128]{2,1,0:T(8,128)(2,1)} %get-tuple-element.15.refs_9_), calls=%async_computation.1 | async-start | bytes 1048576 | tf_op jit(solution)/shard_map/all_to_all | solution.py:207
  127.5 14.4 %all-to-all-done.1 = bf16[8,256,128]{2,1,0:T(8,128)(2,1)} async-done(((bf16[8,256,128]{2,1,0:T(8,128)(2,1)}), bf16[8,256,128]{2,1,0:T(8,128)(2,1)}, u32[]{:S(2)}, u32[]{:S(2)}) %all-to-all-start.1) | async-done | bytes 524320 | tf_op jit(solution)/shard_map/all_to_all | solution.py:207
  141.9 7.7 %all-to-all-start.4 = ((bf16[16,32,1024]{2,1,0:T(8,128)(2,1)}), bf16[16,32,1024]{2,1,0:T(8,128)(2,1)}, u32[]{:S(2)}, u32[]{:S(2)}) async-start(bf16[16,32,1024]{2,1,0:T(8,128)(2,1)} %fusion.5), calls=%async_computation.4 | async-start | bytes 2097152 | tf_op jit(solution)/shard_map/all_to_all | solution.py:207
  151.8 19.0 %attend_backward.1 = (bf16[8,256,128]{2,1,0:T(8,128)(2,1)}, bf16[16,32,256]{2,1,0:T(8,128)(2,1)S(1)}, bf16[16,32,256]{2,1,0:T(8,128)(2,1)S(1)}) custom-call(s32[2]{0:T(128)S(1)} %pad_add_fusion.refs_0_, bf16[256,1024]{1,0:T(8,128)(2,1)S(1)} %fusion.20.refs_1_, bf16[256,1024]{1,0:T(8,128)(2,1)S(1)} %copy-done.6, ...), custom_call_target="tpu_custom_call" | custom-call | flops 11811160064 | bytes 12582912 | tf_op jit(solution)/shard_map/attend_backward/pallas_call | solution.py:171
  173.9 3.6 %all-to-all-start.2 = ((bf16[8,256,128]{2,1,0:T(8,128)(2,1)}), bf16[8,256,128]{2,1,0:T(8,128)(2,1)S(1)}, u32[]{:S(2)}, u32[]{:S(2)}) async-start(bf16[8,256,128]{2,1,0:T(8,128)(2,1)} %get-tuple-element.21), calls=%async_computation.2 | async-start | bytes 1048576 | tf_op jit(solution)/shard_map/all_to_all | solution.py:207
  186.0 8.8 %all-to-all-done.2 = bf16[8,256,128]{2,1,0:T(8,128)(2,1)S(1)} async-done(((bf16[8,256,128]{2,1,0:T(8,128)(2,1)}), bf16[8,256,128]{2,1,0:T(8,128)(2,1)S(1)}, u32[]{:S(2)}, u32[]{:S(2)}) %all-to-all-start.2) | async-done | bytes 524320 | tf_op jit(solution)/shard_map/all_to_all | solution.py:207
  194.8 3.4 %all-to-all-start.5 = ((bf16[8,32,128]{2,1,0:T(8,128)(2,1)}), bf16[8,32,128]{2,1,0:T(8,128)(2,1)S(1)}, u32[]{:S(2)}, u32[]{:S(2)}) async-start(bf16[8,32,128]{2,1,0:T(8,128)(2,1)} %copy.93), calls=%async_computation.5 | async-start | bytes 131072 | tf_op jit(solution)/shard_map/all_to_all | solution.py:207
  200.1 6.4 %all-to-all-done.5 = bf16[8,32,128]{2,1,0:T(8,128)(2,1)S(1)} async-done(((bf16[8,32,128]{2,1,0:T(8,128)(2,1)}), bf16[8,32,128]{2,1,0:T(8,128)(2,1)S(1)}, u32[]{:S(2)}, u32[]{:S(2)}) %all-to-all-start.5) | async-done | bytes 65568 | tf_op jit(solution)/shard_map/all_to_all | solution.py:207
  206.5 7.2 %all-to-all-start.3 = ((bf16[16,96,256]{2,1,0:T(8,128)(2,1)}), bf16[16,96,256]{2,1,0:T(8,128)(2,1)S(1)}, u32[]{:S(2)}, u32[]{:S(2)}) async-start(bf16[16,96,256]{2,1,0:T(8,128)(2,1)} %pad_maximum_fusion), calls=%async_computation.3 | async-start | bytes 1572864 | tf_op jit(solution)/shard_map/all_to_all | solution.py:207
  226.1 4.1 %all-to-all-start.6 = ((bf16[8,224,128]{2,1,0:T(8,128)(2,1)}), bf16[8,224,128]{2,1,0:T(8,128)(2,1)}, u32[]{:S(2)}, u32[]{:S(2)}) async-start(bf16[8,224,128]{2,1,0:T(8,128)(2,1)} %broadcast_in_dim.5), calls=%async_computation.6 | async-start | bytes 917504 | tf_op jit(solution)/shard_map/all_to_all | solution.py:207
  233.8 10.4 %all-to-all-done.6 = bf16[8,224,128]{2,1,0:T(8,128)(2,1)} async-done(((bf16[8,224,128]{2,1,0:T(8,128)(2,1)}), bf16[8,224,128]{2,1,0:T(8,128)(2,1)}, u32[]{:S(2)}, u32[]{:S(2)}) %all-to-all-start.6) | async-done | bytes 458784 | tf_op jit(solution)/shard_map/all_to_all | solution.py:207
  (138 shorter events, 72.7 us)
Async XLA Ops:
  0.6 64.2 %copy-start = (bf16[512,1024]{1,0:T(8,128)(2,1)S(1)}, bf16[512,1024]{1,0:T(8,128)(2,1)}, u32[]{:S(2)}) copy-start(bf16[512,1024]{1,0:T(8,128)(2,1)} %param.13) | copy-start | bytes 3145732
  3.2 17.9 %collective-permute-start = (bf16[256,1024]{1,0:T(8,128)(2,1)S(1)}, bf16[256,1024]{1,0:T(8,128)(2,1)S(1)}, u32[]{:S(2)}, u32[]{:S(2)}) collective-permute-start(bf16[256,1024]{1,0:T(8,128)(2,1)S(1)} %fusion.20.refs_1_), channel_id=1, source_target_pairs={{0,1},{1,2},{2,3},{3,4},{4,5},{5,6},{6,7},{7,0},{8,9},{9,10},{10,1... | collective-permute-start | bytes 1572872 | tf_op jit(solution)/shard_map/ppermute | solution.py:211
  5.2 15.9 %collective-permute-start.4 = (bf16[256,1024]{1,0:T(8,128)(2,1)S(1)}, bf16[256,1024]{1,0:T(8,128)(2,1)S(1)}, u32[]{:S(2)}, u32[]{:S(2)}) collective-permute-start(bf16[256,1024]{1,0:T(8,128)(2,1)S(1)} %fusion.20.refs_1_), channel_id=1, source_target_pairs={{1,0},{2,1},{3,2},{4,3},{5,4},{6,5},{7,6},{0,7},{9,8},{10,9},{11,1... | collective-permute-start | bytes 1572872 | tf_op jit(solution)/shard_map/ppermute | solution.py:215
  21.1 19.0 %copy-start.4 = (bf16[256,1024]{1,0:T(8,128)(2,1)}, bf16[256,1024]{1,0:T(8,128)(2,1)S(1)}, u32[]{:S(2)}) copy-start(bf16[256,1024]{1,0:T(8,128)(2,1)S(1)} %collective-permute-done.refs_2_) | copy-start | bytes 1572868
  21.1 14.4 %collective-permute-start.1 = (bf16[256,1024]{1,0:T(8,128)(2,1)S(1)}, bf16[256,1024]{1,0:T(8,128)(2,1)}, u32[]{:S(2)}, u32[]{:S(2)}) collective-permute-start(bf16[256,1024]{1,0:T(8,128)(2,1)S(1)} %collective-permute-done.refs_2_), channel_id=1, source_target_pairs={{0,1},{1,2},{2,3},{3,4},{4,5},{5,6},{6,7},{7,0},{8,9},{9,10},{10,1... | collective-permute-start | bytes 1572872 | tf_op jit(solution)/shard_map/ppermute | solution.py:211
  21.1 19.0 %copy-start.7 = (bf16[256,1024]{1,0:T(8,128)(2,1)}, bf16[256,1024]{1,0:T(8,128)(2,1)S(1)}, u32[]{:S(2)}) copy-start(bf16[256,1024]{1,0:T(8,128)(2,1)S(1)} %collective-permute-done.4.refs_8_) | copy-start | bytes 1572868
  21.1 14.4 %collective-permute-start.5 = (bf16[256,1024]{1,0:T(8,128)(2,1)S(1)}, bf16[256,1024]{1,0:T(8,128)(2,1)}, u32[]{:S(2)}, u32[]{:S(2)}) collective-permute-start(bf16[256,1024]{1,0:T(8,128)(2,1)S(1)} %collective-permute-done.4.refs_8_), channel_id=1, source_target_pairs={{1,0},{2,1},{3,2},{4,3},{5,4},{6,5},{7,6},{0,7},{9,8},{10,9},{11,1... | collective-permute-start | bytes 1572872 | tf_op jit(solution)/shard_map/ppermute | solution.py:215
  58.1 21.7 %collective-permute-start.2 = (bf16[256,1024]{1,0:T(8,128)(2,1)}, bf16[256,1024]{1,0:T(8,128)(2,1)S(1)}, u32[]{:S(2)}, u32[]{:S(2)}) collective-permute-start(bf16[256,1024]{1,0:T(8,128)(2,1)} %collective-permute-done.1.refs_3_), channel_id=1, source_target_pairs={{0,1},{1,2},{2,3},{3,4},{4,5},{5,6},{6,7},{7,0},{8,9},{9,10},{10,1... | collective-permute-start | bytes 1572872 | tf_op jit(solution)/shard_map/ppermute | solution.py:211
  59.2 22.8 %collective-permute-start.6 = (bf16[256,1024]{1,0:T(8,128)(2,1)}, bf16[256,1024]{1,0:T(8,128)(2,1)S(1)}, u32[]{:S(2)}, u32[]{:S(2)}) collective-permute-start(bf16[256,1024]{1,0:T(8,128)(2,1)} %collective-permute-done.5.refs_7_), channel_id=1, source_target_pairs={{1,0},{2,1},{3,2},{4,3},{5,4},{6,5},{7,6},{0,7},{9,8},{10,9},{11,1... | collective-permute-start | bytes 1572872 | tf_op jit(solution)/shard_map/ppermute | solution.py:215
  62.8 26.0 %collective-permute-start.8 = (bf16[2,128,1024]{2,1,0:T(8,128)(2,1)}, bf16[2,128,1024]{2,1,0:T(8,128)(2,1)}, u32[]{:S(2)}, u32[]{:S(2)}) collective-permute-start(bf16[2,128,1024]{2,1,0:T(8,128)(2,1)} %get-tuple-element.30), channel_id=1, source_target_pairs={{1,0},{2,1},{3,2},{4,3},{5,4},{6,5},{7,6},{0,7},{9,8},{10,9},{11,1... | collective-permute-start | bytes 1572872 | tf_op jit(solution)/shard_map/ppermute | solution.py:215
  64.7 24.1 %collective-permute-start.9 = (bf16[2,128,1024]{2,1,0:T(8,128)(2,1)}, bf16[2,128,1024]{2,1,0:T(8,128)(2,1)}, u32[]{:S(2)}, u32[]{:S(2)}) collective-permute-start(bf16[2,128,1024]{2,1,0:T(8,128)(2,1)} %get-tuple-element.31), channel_id=1, source_target_pairs={{0,1},{1,2},{2,3},{3,4},{4,5},{5,6},{6,7},{7,0},{8,9},{9,10},{10,1... | collective-permute-start | bytes 1572872 | tf_op jit(solution)/shard_map/ppermute | solution.py:211
  66.5 29.3 %all-to-all-start = ((bf16[8,128,128]{2,1,0:T(8,128)(2,1)}), bf16[8,128,128]{2,1,0:T(8,128)(2,1)S(1)}, u32[]{:S(2)}, u32[]{:S(2)}) async-start(bf16[8,128,128]{2,1,0:T(8,128)(2,1)} %copy.81), calls=%async_computation | async-start | bytes 524288 | tf_op jit(solution)/shard_map/all_to_all | solution.py:207
  79.9 14.3 %collective-permute-start.3 = (bf16[128,1024]{1,0:T(8,128)(2,1)S(1)}, bf16[128,1024]{1,0:T(8,128)(2,1)S(1)}, u32[]{:S(2)}, u32[]{:S(2)}) collective-permute-start(bf16[128,1024]{1,0:T(8,128)(2,1)S(1)} %slice.89), channel_id=1, source_target_pairs={{0,1},{1,2},{2,3},{3,4},{4,5},{5,6},{6,7},{7,0},{8,9},{9,10},{10,1... | collective-permute-start | bytes 786440 | tf_op jit(solution)/shard_map/ppermute | solution.py:211
  82.0 12.9 %collective-permute-start.7 = (bf16[128,1024]{1,0:T(8,128)(2,1)S(1)}, bf16[128,1024]{1,0:T(8,128)(2,1)S(1)}, u32[]{:S(2)}, u32[]{:S(2)}) collective-permute-start(bf16[128,1024]{1,0:T(8,128)(2,1)S(1)} %slice.90), channel_id=1, source_target_pairs={{1,0},{2,1},{3,2},{4,3},{5,4},{6,5},{7,6},{0,7},{9,8},{10,9},{11,1... | collective-permute-start | bytes 786440 | tf_op jit(solution)/shard_map/ppermute | solution.py:215
  92.7 31.8 %collective-permute-start.12 = (bf16[16,32,1024]{2,1,0:T(8,128)(2,1)}, bf16[16,32,1024]{2,1,0:T(8,128)(2,1)}, u32[]{:S(2)}, u32[]{:S(2)}) collective-permute-start(bf16[16,32,1024]{2,1,0:T(8,128)(2,1)} %dynamic-slice_bitcast_fusion), channel_id=1, source_target_pairs={{0,8},{8,0},{1,9},{9,1},{2,10},{10,2},{3,11},{11,3},{4,12},{12,4},... | collective-permute-start | bytes 3145736 | tf_op jit(solution)/shard_map/ppermute | solution.py:228
  118.5 23.4 %all-to-all-start.1 = ((bf16[8,256,128]{2,1,0:T(8,128)(2,1)}), bf16[8,256,128]{2,1,0:T(8,128)(2,1)}, u32[]{:S(2)}, u32[]{:S(2)}) async-start(bf16[8,256,128]{2,1,0:T(8,128)(2,1)} %get-tuple-element.15.refs_9_), calls=%async_computation.1 | async-start | bytes 1048576 | tf_op jit(solution)/shard_map/all_to_all | solution.py:207
  124.5 25.2 %copy-start.3 = (bf16[256,1024]{1,0:T(8,128)(2,1)S(1)}, bf16[256,1024]{1,0:T(8,128)(2,1)}, u32[]{:S(2)}) copy-start(bf16[256,1024]{1,0:T(8,128)(2,1)} %copy-done.1) | copy-start | bytes 1572868
  141.9 32.0 %all-to-all-start.4 = ((bf16[16,32,1024]{2,1,0:T(8,128)(2,1)}), bf16[16,32,1024]{2,1,0:T(8,128)(2,1)}, u32[]{:S(2)}, u32[]{:S(2)}) async-start(bf16[16,32,1024]{2,1,0:T(8,128)(2,1)} %fusion.5), calls=%async_computation.4 | async-start | bytes 2097152 | tf_op jit(solution)/shard_map/all_to_all | solution.py:207
  173.9 20.9 %all-to-all-start.2 = ((bf16[8,256,128]{2,1,0:T(8,128)(2,1)}), bf16[8,256,128]{2,1,0:T(8,128)(2,1)S(1)}, u32[]{:S(2)}, u32[]{:S(2)}) async-start(bf16[8,256,128]{2,1,0:T(8,128)(2,1)} %get-tuple-element.21), calls=%async_computation.2 | async-start | bytes 1048576 | tf_op jit(solution)/shard_map/all_to_all | solution.py:207
  179.0 3.1 %collective-permute-start.11 = (bf16[16,16,1024]{2,1,0:T(8,128)(2,1)}, bf16[16,16,1024]{2,1,0:T(8,128)(2,1)}, u32[]{:S(2)}, u32[]{:S(2)}) collective-permute-start(bf16[16,16,1024]{2,1,0:T(8,128)(2,1)} %dynamic-slice_bitcast_fusion.1), channel_id=1, source_target_pairs={{0,8},{8,0},{1,9},{9,1},{2,10},{10,2},{3,11},{11,3},{4,12},{12,4},... | collective-permute-start | bytes 1572872 | tf_op jit(solution)/shard_map/ppermute | solution.py:228
  179.2 2.1 collective-permute-start.10
  194.8 11.7 %all-to-all-start.5 = ((bf16[8,32,128]{2,1,0:T(8,128)(2,1)}), bf16[8,32,128]{2,1,0:T(8,128)(2,1)S(1)}, u32[]{:S(2)}, u32[]{:S(2)}) async-start(bf16[8,32,128]{2,1,0:T(8,128)(2,1)} %copy.93), calls=%async_computation.5 | async-start | bytes 131072 | tf_op jit(solution)/shard_map/all_to_all | solution.py:207
  206.5 18.6 %all-to-all-start.3 = ((bf16[16,96,256]{2,1,0:T(8,128)(2,1)}), bf16[16,96,256]{2,1,0:T(8,128)(2,1)S(1)}, u32[]{:S(2)}, u32[]{:S(2)}) async-start(bf16[16,96,256]{2,1,0:T(8,128)(2,1)} %pad_maximum_fusion), calls=%async_computation.3 | async-start | bytes 1572864 | tf_op jit(solution)/shard_map/all_to_all | solution.py:207
  226.1 18.1 %all-to-all-start.6 = ((bf16[8,224,128]{2,1,0:T(8,128)(2,1)}), bf16[8,224,128]{2,1,0:T(8,128)(2,1)}, u32[]{:S(2)}, u32[]{:S(2)}) async-start(bf16[8,224,128]{2,1,0:T(8,128)(2,1)} %broadcast_in_dim.5), calls=%async_computation.6 | async-start | bytes 917504 | tf_op jit(solution)/shard_map/all_to_all | solution.py:207
  (20 other events, 56.1 us)
